TPU v7x, 128 devices: a whole 4x4x4 slice. The times are simulated.
128 devices in a mesh: ty: 16 (over x, y), tx: 8 (over z, core).
Axes of the slice: x: 4, y: 4, z: 4, core: 2. Of those that a mesh axis runs over, the one named last changes fastest.
Arguments:
- tracers: float32 [3, 60, 256, 2048], P(None, None, 'ty', 'tx'), may hold values from -6 to 6
- courant: float32 [2, 60, 256, 2048], P(None, None, 'ty', 'tx'), may hold values from -0.5 to 0.5
- depth_levels: int32 [256, 2048], P('ty', 'tx'), may hold values from 0 to 60
- mix_inverse: bfloat16 [4, 15, 15, 256, 2048], P(None, None, None, 'ty', 'tx'), may hold values from 0 to 1
- to_ocean: bfloat16 [5, 128, 256, 2048], P(None, None, 'ty', 'tx'), may hold values from -0.3125 to 0.3125
- to_atmos: bfloat16 [5, 128, 256, 2048], P(None, None, 'ty', 'tx'), may hold values from -0.09375 to 0.09375
- atm_flux: bfloat16 [3, 64, 1024], P(None, 'ty', 'tx'), may hold values from -6 to 6
- peer_list: int32 [16, 8, 5], P('ty', 'tx'), may hold values from 0 to 127, as said below
- peer_count: int32 [16, 8, 5], P('ty', 'tx'), may hold values from 1 to 128, as said below
- send_count: int32 [16, 8, 128], P('ty', 'tx'), may hold values from 0 to 128, as said below
- slot_cell: int32 [16, 8, 128, 128], P('ty', 'tx'), may hold values from 0 to 511, as said below
Outputs:
- tracers_out: float32 [3, 60, 256, 2048], P(None, None, 'ty', 'tx')
- surface_temp: float32 [64, 1024], P('ty', 'tx')
Inputs may be any that keep to these rules, and one draw needn't show every extreme that they name: `peer_list`: entry 0 of device d is d itself; entries 1 and 2 are the devices of the same ty index whose tx index is one more and one less, modulo 8; entry 3 is a device of the next ty index and entry 4 one of the previous ty index, both modulo 16, whose tx index differs from d's by 1 or 0 modulo 8. `peer_count`: the largest value, 128, occurs in every draw. send_count[e, d] equals peer_count[d, p] where peer_list[d, p] = e, and 0 where e is not among d's peers. `slot_cell`: slots at or beyond the count hold arbitrary valid cells; a cell may appear in several slots.
All inputs are finite; a program needn't handle non-finite values.
Results may differ from a plain program's by a relative error of at most 0.014.
Values may be sent and summed in bfloat16 or wider, within the bound.
A program may use at most 256 MiB of HBM per device.

v0:
```python
import functools

import jax
import jax.numpy as jnp
from jax import lax
from jax.experimental import pallas as pl
from jax.experimental.pallas import tpu as pltpu
from jax.sharding import PartitionSpec as P

MESH = pl.DeviceIdType.MESH
F32 = jnp.float32
BF16 = jnp.bfloat16
I32 = jnp.int32
SUBSTEPS = 2
LANES = 128
RIM = 32
ROWS = 256
RGROUP = 5
NEAR = tuple((di, dj) for di in (-1, 0, 1) for dj in (-1, 0, 1))


def iota(shape, dim):
    return lax.broadcasted_iota(I32, shape, dim)


def stencil(d):
    return jnp.where((d == 0) | (d == 1), 7.0, jnp.where((d == -1) | (d == 2), -1.0, 0.0))


def nn(a, b):
    return jnp.dot(a, b, preferred_element_type=F32)


def nt(a, b):
    return lax.dot_general(a, b, (((1,), (1,)), ((), ())), preferred_element_type=F32)


def tn(a, b):
    return lax.dot_general(a, b, (((0,), (0,)), ((), ())), preferred_element_type=F32)


def kernel(
    nty,
    ntx,
    tracers,
    courant,
    mix,
    to_ocean,
    to_atmos,
    depth,
    atm,
    slot_cell,
    peer_list,
    peer_count,
    send_count,
    out,
    surf_out,
    q,
    cour,
    mixv,
    toc,
    toa,
    fld,
    sr,
    hr,
    sc,
    hc,
    coef,
    ux,
    uy,
    mv,
    forc,
    depx,
    dr,
    dc,
    c_x,
    c_xh,
    c_xs,
    c_xsh,
    c_y,
    c_yh,
    c_ys,
    c_ysh,
    c_sel,
    c_selc,
    c_e,
    oh,
    flat,
    pk_s,
    pk_r,
    rt_s,
    rt_r,
    s_tr,
    s_co,
    s_mix,
    s_toc,
    s_toa,
    s_out,
    row_ss,
    row_rs,
    col_ss,
    col_rs,
    dep_ss,
    dep_rs,
    pk_ss,
    pk_rs,
    rt_ss,
    rt_rs,
):
    ntr, nb, zb, oy, ox = q.shape
    peers, slots = to_ocean.shape[0], to_ocean.shape[1]
    i = lax.axis_index("ty")
    j = lax.axis_index("tx")

    def device(di, dj):
        return (lax.rem(i + di + nty, nty), lax.rem(j + dj + ntx, ntx))

    barrier = pltpu.get_barrier_semaphore()
    for di, dj in NEAR:
        if (di, dj) != (0, 0):
            pl.semaphore_signal(barrier, inc=1, device_id=device(di, dj), device_id_type=MESH)

    order = tuple((n + 1) % nb for n in range(nb))
    loads = {}
    for b in order:
        loads["tr", b] = pltpu.make_async_copy(
            tracers.at[:, pl.ds(b * zb, zb)], q.at[:, b], s_tr.at[b]
        )
        loads["co", b] = pltpu.make_async_copy(
            courant.at[:, pl.ds(b * zb, zb)], cour.at[:, b], s_co.at[b]
        )
        loads["tr", b].start()
        loads["co", b].start()
    for b in order[:-1]:
        pltpu.make_async_copy(mix.at[b], mixv.at[b], s_mix.at[b]).start()
    pltpu.make_async_copy(to_ocean, toc, s_toc).start()
    pltpu.make_async_copy(mix.at[order[-1]], mixv.at[order[-1]], s_mix.at[order[-1]]).start()
    pltpu.make_async_copy(to_atmos, toa, s_toa).start()

    g = iota((ox, 2 * ox), 0)
    n = iota((ox, 2 * ox), 1)
    d = g - jnp.where(n < ox, n, n - ox - 1)
    c_x[...] = stencil(d).astype(BF16)
    c_xs[...] = jnp.where(d == jnp.where(n < ox, 1, 0), 1.0, 0.0).astype(BF16)
    r = iota((16, 2 * ox), 0)
    n = iota((16, 2 * ox), 1)
    x = jnp.where(n < ox, n, n - ox - 1)
    for f in range(4):
        at = jnp.where(r < 8, -2 + r - 2 * f, ox + r - 8 - 2 * f)
        mine = ((r & 7) >> 1) == f
        if f < 3:
            c_xh[f] = jnp.where(mine, stencil(at - x), 0.0).astype(BF16)
        else:
            hit = mine & (at - x == jnp.where(n < ox, 1, 0))
            c_xsh[...] = jnp.where(hit, 1.0, 0.0).astype(BF16)
    m = iota((2 * ROWS, ROWS), 0)
    n = iota((2 * ROWS, ROWS), 1)
    mm = jnp.where(m < ROWS, m, m - ROWS)
    y = jnp.where(m < ROWS, mm & 15, (mm & 15) - 1)
    d = (n & 15) - y
    same = (mm >> 4) == (n >> 4)
    c_y[...] = jnp.where(same, stencil(d), 0.0).astype(BF16)
    hit = same & (d == jnp.where(m < ROWS, 1, 0))
    c_ys[...] = jnp.where(hit, 1.0, 0.0).astype(BF16)
    m = iota((2 * ROWS, 2 * RIM), 0)
    n = iota((2 * ROWS, 2 * RIM), 1)
    mm = jnp.where(m < ROWS, m, m - ROWS)
    y = jnp.where(m < ROWS, mm & 15, (mm & 15) - 1)
    nn_ = jnp.where(n < RIM, n, n - RIM)
    d = jnp.where(n < RIM, -2 + (nn_ & 1), oy + (nn_ & 1)) - y
    same = (mm >> 4) == (nn_ >> 1)
    c_yh[...] = jnp.where(same, stencil(d), 0.0).astype(BF16)
    hit = same & (d == jnp.where(m < ROWS, 1, 0))
    c_ysh[...] = jnp.where(hit, 1.0, 0.0).astype(BF16)
    m = iota((2 * RIM, ROWS), 0)
    n = iota((2 * RIM, ROWS), 1)
    mm = jnp.where(m < RIM, m, m - RIM)
    y = jnp.where(m < RIM, oy - 2 + (mm & 1), mm & 1)
    open_down = jnp.where(i == nty - 1, 0.0, 1.0)
    open_up = jnp.where(i == 0, 0.0, 1.0)
    hit = ((mm >> 1) == (n >> 4)) & ((n & 15) == y)
    c_sel[...] = jnp.where(hit, jnp.where(m < RIM, open_down, open_up), 0.0).astype(BF16)
    r = iota((16, ox), 0)
    n = iota((16, ox), 1)
    open_right = jnp.where(j == ntx - 1, 0.0, 1.0)
    open_left = jnp.where(j == 0, 0.0, 1.0)
    for f in range(4):
        at = jnp.where(r < 8, ox - 2 + r - 2 * f, r - 8 - 2 * f)
        mine = ((r & 7) >> 1) == f
        hit = mine & (at == n)
        c_selc[f] = jnp.where(hit, jnp.where(r < 8, open_right, open_left), 0.0).astype(BF16)
    r = iota((slots, slots * oy), 0)
    n = iota((slots, slots * oy), 1)
    c_e[...] = jnp.where((n >> 4) == r, 1.0, 0.0).astype(BF16)

    cells = iota((oh.shape[0], slots), 0)
    for k, (di, dj) in enumerate(NEAR):
        ti, tj = device(di, dj)
        row = slot_cell[0, 0, pl.ds(ti * ntx + tj, 1), :]
        oh[:, k * slots : (k + 1) * slots] = jnp.where(cells == row, 1.0, 0.0).astype(BF16)
    flux = atm[...].astype(F32)
    flat[...] = jnp.zeros_like(flat)
    for c in range(flux.shape[0]):
        for r in range(flux.shape[1]):
            flat[c : c + 1, r * LANES : (r + 1) * LANES] = flux[c, r : r + 1, :]
    picks = nn(flat[...].astype(BF16), oh[...])
    for k in range(len(NEAR)):
        pk_s[k] = picks[:, k * slots : (k + 1) * slots]

    pl.semaphore_wait(barrier, len(NEAR) - 1)

    def depth_copies():
        return (
            pltpu.make_async_remote_copy(
                depth.at[pl.ds(oy - 8, 8)], dr.at[0], dep_ss.at[0], dep_rs.at[0],
                device_id=device(1, 0), device_id_type=MESH,
            ),
            pltpu.make_async_remote_copy(
                depth.at[pl.ds(0, 8)], dr.at[1], dep_ss.at[1], dep_rs.at[1],
                device_id=device(-1, 0), device_id_type=MESH,
            ),
            pltpu.make_async_remote_copy(
                depth.at[:, pl.ds(ox - LANES, LANES)], dc.at[0], dep_ss.at[2], dep_rs.at[2],
                device_id=device(0, 1), device_id_type=MESH,
            ),
            pltpu.make_async_remote_copy(
                depth.at[:, pl.ds(0, LANES)], dc.at[1], dep_ss.at[3], dep_rs.at[3],
                device_id=device(0, -1), device_id_type=MESH,
            ),
        )

    def near_copies(source, target, ss, rs, of):
        made = []
        for k, (di, dj) in enumerate(NEAR):
            if (di, dj) != (0, 0):
                made.append(
                    pltpu.make_async_remote_copy(
                        source.at[of(k, di, dj)], target.at[len(NEAR) - 1 - k], ss.at[k],
                        rs.at[len(NEAR) - 1 - k], device_id=device(di, dj), device_id_type=MESH,
                    )
                )
        return made

    def rim_copies(step, b, fields):
        rows = [
            pltpu.make_async_remote_copy(
                sr.at[step, b, pl.ds(0, fields), pl.ds(s * RIM, RIM)],
                hr.at[step, b, pl.ds(0, fields), pl.ds(s * RIM, RIM)],
                row_ss.at[step, s, b], row_rs.at[step, s, b],
                device_id=device(1 - 2 * s, 0), device_id_type=MESH,
            )
            for s in range(2)
        ]
        cols = [
            pltpu.make_async_remote_copy(
                sc.at[step, b, pl.ds(s * 8, 8)],
                hc.at[step, b, pl.ds(s * 8, 8)],
                col_ss.at[step, s, b], col_rs.at[step, s, b],
                device_id=device(0, 1 - 2 * s), device_id_type=MESH,
            )
            for s in range(2)
        ]
        return rows + cols

    for copy in depth_copies():
        copy.start()
    for copy in near_copies(pk_s, pk_r, pk_ss, pk_rs, lambda k, di, dj: k):
        copy.start()

    dep = depth[...]

    def pack(step, b, row_fields, col_fields):
        for f, source in enumerate(row_fields):
            sr[step, b, f] = nn(c_sel[...], fld[source, b]).astype(BF16)
        cols = nt(c_selc[0], fld[col_fields[0], b])
        for f in range(1, len(col_fields)):
            cols = cols + nt(c_selc[f], fld[col_fields[f], b])
        sc[step, b] = cols
        for copy in rim_copies(step, b, len(row_fields)):
            copy.start()

    def fill(idx, carry):
        b = lax.rem(idx + 1, nb)
        pltpu.make_async_copy(tracers.at[:, pl.ds(0, zb)], q.at[:, b], s_tr.at[b]).wait()
        pltpu.make_async_copy(courant.at[:, pl.ds(0, zb)], cour.at[:, b], s_co.at[b]).wait()

        def level(k, carry):
            rows = pl.ds(pl.multiple_of(k * oy, oy), oy)
            for t in range(ntr):
                fld[t, b, rows, :] = q[t, b, k].astype(BF16)
            wet = (b * zb + k) < dep
            for a in range(2):
                fld[ntr + a, b, rows, :] = jnp.where(wet, cour[a, b, k], 0.0).astype(BF16)
            return carry

        lax.fori_loop(0, zb, level, 0)
        for f in range(ntr + 2):
            fld[f, b, zb * oy :, :] = jnp.zeros((ROWS - zb * oy, ox), BF16)
        pack(0, b, (0, 1, 2, 4), (0, 1, 2, 3))
        return carry

    lax.fori_loop(0, nb, fill, 0)

    for copy in depth_copies():
        copy.wait()
    south = jnp.where(i == 0, 0, dr[0])
    north = jnp.where(i == nty - 1, 0, dr[1])
    west = jnp.where(j == 0, 0, dc[0])
    east = jnp.where(j == ntx - 1, 0, dc[1])
    wide = jnp.concatenate([dep, east], axis=1)
    depx[0] = pltpu.roll(wide, ox + LANES - 1, 1)[:, :ox]
    wide = jnp.concatenate([west, dep], axis=1)
    depx[1] = pltpu.roll(wide, 1, 1)[:, LANES:]
    tall = jnp.concatenate([dep, north], axis=0)
    depx[2] = pltpu.roll(tall, oy + 7, 0)[:oy]
    tall = jnp.concatenate([south, dep], axis=0)
    depx[3] = pltpu.roll(tall, 1, 0)[8:]

    def wait_rims(step, b, fields):
        for copy in rim_copies(step, b, fields):
            copy.wait()

    def faces(b):
        ux[0] = nn(fld[ntr, b], c_xs[...]) + tn(hc[0, b].astype(BF16), c_xsh[...])
        uy[0] = nn(c_ys[...], fld[ntr + 1, b]) + nn(c_ysh[...], hr[0, b, ntr])

        def level(k, carry):
            rows = pl.ds(pl.multiple_of(k * oy, oy), oy)
            later = pl.ds(pl.multiple_of(ROWS + k * oy, oy), oy)
            at = b * zb + k
            wet = at < dep
            own = jnp.where(wet, cour[0, b, k] * (1.0 / 24.0), 0.0)
            coef[0, b, k] = jnp.where(at < depx[0], own, 0.0) + jnp.where(
                wet, ux[0, rows, 0:ox] * (1.0 / 24.0), 0.0
            )
            coef[1, b, k] = jnp.where(at < depx[1], own, 0.0) + jnp.where(
                wet, ux[0, rows, ox : 2 * ox] * (1.0 / 24.0), 0.0
            )
            own = jnp.where(wet, cour[1, b, k] * (1.0 / 24.0), 0.0)
            coef[2, b, k] = jnp.where(at < depx[2], own, 0.0) + jnp.where(
                wet, uy[0, rows, :] * (1.0 / 24.0), 0.0
            )
            coef[3, b, k] = jnp.where(at < depx[3], own, 0.0) + jnp.where(
                wet, uy[0, later, :] * (1.0 / 24.0), 0.0
            )
            return carry

        lax.fori_loop(0, zb, level, 0)

    def advect(step, b):
        halo = hc[step, b].astype(BF16)
        for t in range(ntr):
            ux[t] = nn(fld[t, b], c_x[...]) + tn(halo, c_xh[t])
            uy[t] = nn(c_y[...], fld[t, b]) + nn(c_yh[...], hr[step, b, t])

        def level(k, carry):
            rows = pl.ds(pl.multiple_of(k * oy, oy), oy)
            later = pl.ds(pl.multiple_of(ROWS + k * oy, oy), oy)
            wet = (b * zb + k) < dep
            c0, c1, c2, c3 = (coef[a, b, k] for a in range(4))
            for t in range(ntr):
                moved = jnp.where(wet, q[t, b, k], 0.0)
                moved = moved - (c0 * ux[t, rows, 0:ox] - c1 * ux[t, rows, ox : 2 * ox])
                mv[t, k] = moved - (c2 * uy[t, rows, :] - c3 * uy[t, later, :])
            return carry

        lax.fori_loop(0, zb, level, 0)

        @pl.when(b == 0)
        def _():
            for t in range(ntr):
                mv[t, 0] = mv[t, 0] + jnp.where(dep > 0, forc[t], 0.0)

    def mixing(b, keep):
        groups = zb // RGROUP

        def part(idx, carry):
            lanes = pl.ds(pl.multiple_of((idx // groups) * LANES, LANES), LANES)
            first = lax.rem(idx, groups) * RGROUP
            acc = [[None] * ntr for _ in range(RGROUP)]
            for c in range(zb):
                moved = [mv[t, c, :, lanes] for t in range(ntr)]
                for r in range(RGROUP):
                    weight = mixv[b, first + r, c, :, lanes].astype(F32)
                    for t in range(ntr):
                        term = weight * moved[t]
                        acc[r][t] = term if c == 0 else acc[r][t] + term
            for r in range(RGROUP):
                k = first + r
                wet = (b * zb + k) < depth[:, lanes]
                for t in range(ntr):
                    value = jnp.where(wet, acc[r][t], 0.0)
                    q[t, b, k, :, lanes] = value
                    if keep:
                        fld[t, b, pl.ds(pl.multiple_of(k * oy, oy), oy), lanes] = value.astype(BF16)
            return carry

        lax.fori_loop(0, groups * (ox // LANES), part, 0)

    def force():
        for copy in near_copies(pk_s, pk_r, pk_ss, pk_rs, lambda k, di, dj: k):
            copy.wait()
        pltpu.make_async_copy(to_ocean, toc, s_toc).wait()
        mine = pk_s[4]
        chosen = [mine, pk_r[5], pk_r[3]]
        for p, di in ((3, 1), (4, -1)):
            ids = [device(di, dj) for dj in (-1, 0, 1)]
            ids = [a * ntx + b for a, b in ids]
            base = (di + 1) * 3
            e = peer_list[0, 0, p]
            got = jnp.where(e == ids[0], pk_r[base], pk_r[base + 1])
            chosen.append(jnp.where(e == ids[2], pk_r[base + 2], got))
        slot = iota((8, slots), 1)
        y = iota((oy, slots * oy), 0)
        x = iota((oy, slots * oy), 1)
        diagonal = (x & 15) == y
        total = jnp.zeros((ntr * oy, ox), F32)
        for p in range(peers):
            live = jnp.where(slot < peer_count[0, 0, p], chosen[p], 0.0).astype(BF16)
            spread = nn(live, c_e[...])
            left = jnp.concatenate(
                [jnp.where(diagonal, spread[c : c + 1, :], 0.0).astype(BF16) for c in range(ntr)],
                axis=0,
            )
            total = total + nn(left, toc[p].reshape(slots * oy, ox))
        for t in range(ntr):
            forc[t] = total[t * oy : (t + 1) * oy]

    def ret_copies():
        of = lambda k, di, dj: {1: 3, -1: 4}[di] if di != 0 else {1: 1, -1: 2}[dj]
        return near_copies(rt_s, rt_r, rt_ss, rt_rs, of)

    def give_back():
        pltpu.make_async_copy(to_atmos, toa, s_toa).wait()
        surface = q[0, 0, 0].astype(BF16)
        y = iota((oy, slots * oy), 0)
        x = iota((oy, slots * oy), 1)
        diagonal = (x & 15) == y
        for p in range(peers):
            sums = nt(surface, toa[p].reshape(slots * oy, ox))
            sums = jnp.where(diagonal, sums, 0.0)
            high = sums.astype(BF16)
            low = (sums - high.astype(F32)).astype(BF16)
            both = nt(high, c_e[...]) + nt(low, c_e[...])
            rt_s[p] = jnp.broadcast_to(jnp.sum(both, axis=0, keepdims=True), (8, slots))
        for copy in ret_copies():
            copy.start()

    def first_step(idx, carry):
        b = lax.rem(idx + 1, nb)
        wait_rims(0, b, 4)
        faces(b)

        @pl.when(b == 0)
        def _():
            force()

        advect(0, b)
        pltpu.make_async_copy(mix.at[0], mixv.at[b], s_mix.at[b]).wait()
        mixing(b, True)
        pack(1, b, (0, 1, 2), (0, 1, 2))
        return carry

    lax.fori_loop(0, nb, first_step, 0)

    def second_step(idx, carry):
        b = jnp.where(idx < 2, 1 - idx, idx)
        wait_rims(1, b, 3)
        advect(1, b)
        mixing(b, False)
        pltpu.make_async_copy(q.at[:, b], out.at[:, pl.ds(b * zb, zb)], s_out.at[b]).start()

        @pl.when(b == 0)
        def _():
            give_back()

        return carry

    lax.fori_loop(0, nb, second_step, 0)

    for copy in ret_copies():
        copy.wait()
    slot = iota((1, slots), 1)
    parts = []
    for k, (di, dj) in enumerate(NEAR):
        ti, tj = device(di, dj)
        value = rt_s[0] if (di, dj) == (0, 0) else rt_r[k]
        kept = slot < send_count[0, 0, ti * ntx + tj]
        parts.append(jnp.where(kept, value, 0.0))
    values = jnp.concatenate(parts, axis=1)
    high = values.astype(BF16)
    low = (values - high.astype(F32)).astype(BF16)
    landed = nt(high, oh[...]) + nt(low, oh[...])
    for r in range(surf_out.shape[0]):
        surf_out[r : r + 1, :] = landed[0:1, r * LANES : (r + 1) * LANES]
    for b in range(nb):
        pltpu.make_async_copy(q.at[:, b], out.at[:, pl.ds(b * zb, zb)], s_out.at[b]).wait()


def body(
    nty,
    ntx,
    tracers,
    courant,
    depth_levels,
    mix_inverse,
    to_ocean,
    to_atmos,
    atm_flux,
    peer_list,
    peer_count,
    send_count,
    slot_cell,
):
    ntr, levels, oy, ox = tracers.shape
    nb, zb = mix_inverse.shape[:2]
    peers, slots = to_ocean.shape[:2]
    cells = atm_flux.shape[1] * atm_flux.shape[2]
    near = len(NEAR)
    anywhere = pl.BlockSpec(memory_space=pl.ANY)
    vmem = pl.BlockSpec(memory_space=pltpu.VMEM)
    smem = pl.BlockSpec(memory_space=pltpu.SMEM)
    dma = pltpu.SemaphoreType.DMA
    scratch = [
        pltpu.VMEM((ntr, nb, zb, oy, ox), F32),
        pltpu.VMEM((2, nb, zb, oy, ox), F32),
        pltpu.VMEM(mix_inverse.shape, BF16),
        pltpu.VMEM(to_ocean.shape, BF16),
        pltpu.VMEM(to_atmos.shape, BF16),
        pltpu.VMEM((ntr + 2, nb, ROWS, ox), BF16),
        pltpu.VMEM((SUBSTEPS, nb, 4, 2 * RIM, ox), BF16),
        pltpu.VMEM((SUBSTEPS, nb, 4, 2 * RIM, ox), BF16),
        pltpu.VMEM((SUBSTEPS, nb, 16, ox), F32),
        pltpu.VMEM((SUBSTEPS, nb, 16, ox), F32),
        pltpu.VMEM((4, nb, zb, oy, ox), F32),
        pltpu.VMEM((ntr, ROWS, 2 * ox), F32),
        pltpu.VMEM((ntr, 2 * ROWS, ox), F32),
        pltpu.VMEM((ntr, zb, oy, ox), F32),
        pltpu.VMEM((ntr, oy, ox), F32),
        pltpu.VMEM((4, oy, ox), I32),
        pltpu.VMEM((2, 8, ox), I32),
        pltpu.VMEM((2, oy, LANES), I32),
        pltpu.VMEM((ox, 2 * ox), BF16),
        pltpu.VMEM((3, 16, 2 * ox), BF16),
        pltpu.VMEM((ox, 2 * ox), BF16),
        pltpu.VMEM((16, 2 * ox), BF16),
        pltpu.VMEM((2 * ROWS, ROWS), BF16),
        pltpu.VMEM((2 * ROWS, 2 * RIM), BF16),
        pltpu.VMEM((2 * ROWS, ROWS), BF16),
        pltpu.VMEM((2 * ROWS, 2 * RIM), BF16),
        pltpu.VMEM((2 * RIM, ROWS), BF16),
        pltpu.VMEM((4, 16, ox), BF16),
        pltpu.VMEM((slots, slots * oy), BF16),
        pltpu.VMEM((cells, near * slots), BF16),
        pltpu.VMEM((8, cells), F32),
        pltpu.VMEM((near, 8, slots), F32),
        pltpu.VMEM((near, 8, slots), F32),
        pltpu.VMEM((peers, 8, slots), F32),
        pltpu.VMEM((near, 8, slots), F32),
        dma((nb,)),
        dma((nb,)),
        dma((nb,)),
        dma,
        dma,
        dma((nb,)),
        dma((SUBSTEPS, 2, nb)),
        dma((SUBSTEPS, 2, nb)),
        dma((SUBSTEPS, 2, nb)),
        dma((SUBSTEPS, 2, nb)),
        dma((4,)),
        dma((4,)),
        dma((near,)),
        dma((near,)),
        dma((near,)),
        dma((near,)),
    ]
    return pl.pallas_call(
        functools.partial(kernel, nty, ntx),
        out_shape=(
            jax.ShapeDtypeStruct(tracers.shape, F32),
            jax.ShapeDtypeStruct(atm_flux.shape[1:], F32),
        ),
        in_specs=[anywhere] * 5 + [vmem] * 3 + [smem] * 3,
        out_specs=(anywhere, vmem),
        scratch_shapes=scratch,
        compiler_params=pltpu.CompilerParams(
            collective_id=0, has_side_effects=True, vmem_limit_bytes=56 * 1024 * 1024
        ),
        cost_estimate=pl.CostEstimate(flops=10**9, bytes_accessed=26 * 10**6, transcendentals=0),
        name="interval",
    )(
        tracers,
        courant,
        mix_inverse,
        to_ocean,
        to_atmos,
        depth_levels,
        atm_flux,
        slot_cell,
        peer_list,
        peer_count,
        send_count,
    )


def solution(mesh):
    in_specs = (
        P(None, None, "ty", "tx"),
        P(None, None, "ty", "tx"),
        P("ty", "tx"),
        P(None, None, None, "ty", "tx"),
        P(None, None, "ty", "tx"),
        P(None, None, "ty", "tx"),
        P(None, "ty", "tx"),
        P("ty", "tx", None),
        P("ty", "tx", None),
        P("ty", "tx", None),
        P("ty", "tx", None, None),
    )
    out_specs = (P(None, None, "ty", "tx"), P("ty", "tx"))
    part = functools.partial(body, mesh.shape["ty"], mesh.shape["tx"])
    return jax.shard_map(part, mesh=mesh, in_specs=in_specs, out_specs=out_specs, check_vma=False)
```

profile of v0, /device:TPU:0, one launch (start us, length us, event | category | flops | bytes accessed | tf_op | source)
XLA Modules:
  0.0 55.0 jit_solution(7698592029486552802)
XLA Ops:
  0.6 50.1 %interval.1 = (f32[3,60,16,256]{3,2,1,0:T(8,128)}, f32[4,128]{1,0:T(4,128)}) custom-call(f32[3,60,16,256]{3,2,1,0:T(8,128)} %tracers.1, f32[2,60,16,256]{3,2,1,0:T(8,128)} %courant.1, bf16[4,15,15,16,256]{4,3,2,1,0:T(8,128)(2,1)} %mix.1, bf16[5,128,16,256]{3,2,1,0:T(8,128)(2,1)} %to_ocean.1, bf16[5,128,16,256]{3,2,1,0:T(8,128)(2,1)} %to_atmos.1, ...), custom_call_target="tpu_custom_call" | custom-call | flops 1000000000 | bytes 26000000 | tf_op jit(solution)/shard_map/interval/pallas_call | solution.py:577
  50.7 0.0 copy-start
  50.7 3.7 %copy.15 = f32[3,60,16,256]{3,2,1,0:T(8,128)} copy(f32[3,60,16,256]{3,2,1,0:T(8,128)} %get-tuple-element.4) | data formatting | bytes 5898240
  54.5 0.0 copy-done
  54.5 0.6 %copy.16 = f32[4,128]{1,0:T(4,128)} copy(f32[4,128]{1,0:T(4,128)S(1)} %copy-done) | data formatting | bytes 4096
Async XLA Ops:
  50.7 3.7 %copy-start = (f32[4,128]{1,0:T(4,128)S(1)}, f32[4,128]{1,0:T(4,128)}, u32[]{:S(2)}) copy-start(f32[4,128]{1,0:T(4,128)} %get-tuple-element.5) | copy-start | bytes 6148
where the time goes:
time: 55.2 us; the launch traced here: 55 us
  Pallas kernels  50.1 us (91%)
  local copies, waits for them, and re-layouts  4.29 us (8%)
  between operations  0.65 us (1%)
    pallas_call x1, Pallas kernels, body(): pl.pallas_call(functools.partial(kernel, nty, ntx), out_shape=(jax.ShapeD...  50.1 us
    unnamed x4, local copies, waits for them, and re-layouts  4.29 us

commit v1 on v0

--- a/solution.py
+++ b/solution.py
@@ -16,6 +16,7 @@
 RIM = 32
 ROWS = 256
 RGROUP = 5
+CGROUP = 5
 NEAR = tuple((di, dj) for di in (-1, 0, 1) for dj in (-1, 0, 1))
 
 
@@ -47,12 +48,12 @@
     mix,
     to_ocean,
     to_atmos,
-    depth,
-    atm,
-    slot_cell,
-    peer_list,
-    peer_count,
-    send_count,
+    depth_in,
+    atm_in,
+    slot_cell_in,
+    peer_list_in,
+    peer_count_in,
+    send_count_in,
     out,
     surf_out,
     q,
@@ -90,12 +91,18 @@
     pk_r,
     rt_s,
     rt_r,
+    depth,
+    atm,
+    slot_cell,
+    peer_list,
+    peer_count,
+    send_count,
+    s_in,
     s_tr,
     s_co,
     s_mix,
     s_toc,
     s_toa,
-    s_out,
     row_ss,
     row_rs,
     col_ss,
@@ -120,6 +127,20 @@
         if (di, dj) != (0, 0):
             pl.semaphore_signal(barrier, inc=1, device_id=device(di, dj), device_id_type=MESH)
 
+    small = [
+        pltpu.make_async_copy(source, target, s_in.at[k])
+        for k, (source, target) in enumerate(
+            (
+                (depth_in, depth),
+                (slot_cell_in, slot_cell),
+                (atm_in, atm),
+                (peer_list_in, peer_list),
+                (peer_count_in, peer_count),
+                (send_count_in, send_count),
+            )
+        )
+    ]
+    small[0].start()
     order = tuple((n + 1) % nb for n in range(nb))
     loads = {}
     for b in order:
@@ -131,11 +152,130 @@
         )
         loads["tr", b].start()
         loads["co", b].start()
+    for copy in small[1:]:
+        copy.start()
     for b in order[:-1]:
         pltpu.make_async_copy(mix.at[b], mixv.at[b], s_mix.at[b]).start()
     pltpu.make_async_copy(to_ocean, toc, s_toc).start()
     pltpu.make_async_copy(mix.at[order[-1]], mixv.at[order[-1]], s_mix.at[order[-1]]).start()
     pltpu.make_async_copy(to_atmos, toa, s_toa).start()
+
+    m = iota((2 * RIM, ROWS), 0)
+    n = iota((2 * RIM, ROWS), 1)
+    mm = jnp.where(m < RIM, m, m - RIM)
+    y = jnp.where(m < RIM, oy - 2 + (mm & 1), mm & 1)
+    open_down = jnp.where(i == nty - 1, 0.0, 1.0)
+    open_up = jnp.where(i == 0, 0.0, 1.0)
+    hit = ((mm >> 1) == (n >> 4)) & ((n & 15) == y)
+    c_sel[...] = jnp.where(hit, jnp.where(m < RIM, open_down, open_up), 0.0).astype(BF16)
+    r = iota((16, ox), 0)
+    n = iota((16, ox), 1)
+    open_right = jnp.where(j == ntx - 1, 0.0, 1.0)
+    open_left = jnp.where(j == 0, 0.0, 1.0)
+    for f in range(4):
+        at = jnp.where(r < 8, ox - 2 + r - 2 * f, r - 8 - 2 * f)
+        mine = ((r & 7) >> 1) == f
+        hit = mine & (at == n)
+        c_selc[f] = jnp.where(hit, jnp.where(r < 8, open_right, open_left), 0.0).astype(BF16)
+    def depth_copies():
+        return (
+            pltpu.make_async_remote_copy(
+                depth.at[pl.ds(oy - 8, 8)], dr.at[0], dep_ss.at[0], dep_rs.at[0],
+                device_id=device(1, 0), device_id_type=MESH,
+            ),
+            pltpu.make_async_remote_copy(
+                depth.at[pl.ds(0, 8)], dr.at[1], dep_ss.at[1], dep_rs.at[1],
+                device_id=device(-1, 0), device_id_type=MESH,
+            ),
+            pltpu.make_async_remote_copy(
+                depth.at[:, pl.ds(ox - LANES, LANES)], dc.at[0], dep_ss.at[2], dep_rs.at[2],
+                device_id=device(0, 1), device_id_type=MESH,
+            ),
+            pltpu.make_async_remote_copy(
+                depth.at[:, pl.ds(0, LANES)], dc.at[1], dep_ss.at[3], dep_rs.at[3],
+                device_id=device(0, -1), device_id_type=MESH,
+            ),
+        )
+
+    def near_copies(source, target, ss, rs, of):
+        made = []
+        for k, (di, dj) in enumerate(NEAR):
+            if (di, dj) != (0, 0):
+                made.append(
+                    pltpu.make_async_remote_copy(
+                        source.at[of(k, di, dj)], target.at[len(NEAR) - 1 - k], ss.at[k],
+                        rs.at[len(NEAR) - 1 - k], device_id=device(di, dj), device_id_type=MESH,
+                    )
+                )
+        return made
+
+    def rim_copies(step, b, fields):
+        rows = [
+            pltpu.make_async_remote_copy(
+                sr.at[step, b, pl.ds(0, fields), pl.ds(s * RIM, RIM)],
+                hr.at[step, b, pl.ds(0, fields), pl.ds(s * RIM, RIM)],
+                row_ss.at[step, s, b], row_rs.at[step, s, b],
+                device_id=device(1 - 2 * s, 0), device_id_type=MESH,
+            )
+            for s in range(2)
+        ]
+        cols = [
+            pltpu.make_async_remote_copy(
+                sc.at[step, b, pl.ds(s * 8, 8)],
+                hc.at[step, b, pl.ds(s * 8, 8)],
+                col_ss.at[step, s, b], col_rs.at[step, s, b],
+                device_id=device(0, 1 - 2 * s), device_id_type=MESH,
+            )
+            for s in range(2)
+        ]
+        return rows + cols
+
+    small[0].wait()
+    dep = depth[...]
+
+    def pack(step, b, row_fields, col_fields):
+        for f, source in enumerate(row_fields):
+            sr[step, b, f] = nn(c_sel[...], fld[source, b]).astype(BF16)
+        cols = nt(c_selc[0], fld[col_fields[0], b])
+        for f in range(1, len(col_fields)):
+            cols = cols + nt(c_selc[f], fld[col_fields[f], b])
+        sc[step, b] = cols
+
+    def send(step, b, fields):
+        for copy in rim_copies(step, b, fields):
+            copy.start()
+
+    def fill(b):
+        pltpu.make_async_copy(tracers.at[:, pl.ds(0, zb)], q.at[:, b], s_tr.at[b]).wait()
+        pltpu.make_async_copy(courant.at[:, pl.ds(0, zb)], cour.at[:, b], s_co.at[b]).wait()
+
+        def level(k, carry):
+            rows = pl.ds(pl.multiple_of(k * oy, oy), oy)
+            for t in range(ntr):
+                fld[t, b, rows, :] = q[t, b, k].astype(BF16)
+            wet = (b * zb + k) < dep
+            for a in range(2):
+                fld[ntr + a, b, rows, :] = jnp.where(wet, cour[a, b, k], 0.0).astype(BF16)
+            return carry
+
+        lax.fori_loop(0, zb, level, 0)
+        for f in range(ntr + 2):
+            fld[f, b, zb * oy :, :] = jnp.zeros((ROWS - zb * oy, ox), BF16)
+        pack(0, b, (0, 1, 2, 4), (0, 1, 2, 3))
+
+    fill(order[0])
+    pl.semaphore_wait(barrier, len(NEAR) - 1)
+    for copy in depth_copies():
+        copy.start()
+    send(0, order[0], 4)
+
+    def fill_and_send(idx, carry):
+        b = lax.rem(idx + 1, nb)
+        fill(b)
+        send(0, b, 4)
+        return carry
+
+    lax.fori_loop(1, nb, fill_and_send, 0)
 
     g = iota((ox, 2 * ox), 0)
     n = iota((ox, 2 * ox), 1)
@@ -172,26 +312,12 @@
     c_yh[...] = jnp.where(same, stencil(d), 0.0).astype(BF16)
     hit = same & (d == jnp.where(m < ROWS, 1, 0))
     c_ysh[...] = jnp.where(hit, 1.0, 0.0).astype(BF16)
-    m = iota((2 * RIM, ROWS), 0)
-    n = iota((2 * RIM, ROWS), 1)
-    mm = jnp.where(m < RIM, m, m - RIM)
-    y = jnp.where(m < RIM, oy - 2 + (mm & 1), mm & 1)
-    open_down = jnp.where(i == nty - 1, 0.0, 1.0)
-    open_up = jnp.where(i == 0, 0.0, 1.0)
-    hit = ((mm >> 1) == (n >> 4)) & ((n & 15) == y)
-    c_sel[...] = jnp.where(hit, jnp.where(m < RIM, open_down, open_up), 0.0).astype(BF16)
-    r = iota((16, ox), 0)
-    n = iota((16, ox), 1)
-    open_right = jnp.where(j == ntx - 1, 0.0, 1.0)
-    open_left = jnp.where(j == 0, 0.0, 1.0)
-    for f in range(4):
-        at = jnp.where(r < 8, ox - 2 + r - 2 * f, r - 8 - 2 * f)
-        mine = ((r & 7) >> 1) == f
-        hit = mine & (at == n)
-        c_selc[f] = jnp.where(hit, jnp.where(r < 8, open_right, open_left), 0.0).astype(BF16)
     r = iota((slots, slots * oy), 0)
     n = iota((slots, slots * oy), 1)
     c_e[...] = jnp.where((n >> 4) == r, 1.0, 0.0).astype(BF16)
+
+    for copy in small[1:]:
+        copy.wait()
 
     cells = iota((oh.shape[0], slots), 0)
     for k, (di, dj) in enumerate(NEAR):
@@ -207,99 +333,8 @@
     for k in range(len(NEAR)):
         pk_s[k] = picks[:, k * slots : (k + 1) * slots]
 
-    pl.semaphore_wait(barrier, len(NEAR) - 1)
-
-    def depth_copies():
-        return (
-            pltpu.make_async_remote_copy(
-                depth.at[pl.ds(oy - 8, 8)], dr.at[0], dep_ss.at[0], dep_rs.at[0],
-                device_id=device(1, 0), device_id_type=MESH,
-            ),
-            pltpu.make_async_remote_copy(
-                depth.at[pl.ds(0, 8)], dr.at[1], dep_ss.at[1], dep_rs.at[1],
-                device_id=device(-1, 0), device_id_type=MESH,
-            ),
-            pltpu.make_async_remote_copy(
-                depth.at[:, pl.ds(ox - LANES, LANES)], dc.at[0], dep_ss.at[2], dep_rs.at[2],
-                device_id=device(0, 1), device_id_type=MESH,
-            ),
-            pltpu.make_async_remote_copy(
-                depth.at[:, pl.ds(0, LANES)], dc.at[1], dep_ss.at[3], dep_rs.at[3],
-                device_id=device(0, -1), device_id_type=MESH,
-            ),
-        )
-
-    def near_copies(source, target, ss, rs, of):
-        made = []
-        for k, (di, dj) in enumerate(NEAR):
-            if (di, dj) != (0, 0):
-                made.append(
-                    pltpu.make_async_remote_copy(
-                        source.at[of(k, di, dj)], target.at[len(NEAR) - 1 - k], ss.at[k],
-                        rs.at[len(NEAR) - 1 - k], device_id=device(di, dj), device_id_type=MESH,
-                    )
-                )
-        return made
-
-    def rim_copies(step, b, fields):
-        rows = [
-            pltpu.make_async_remote_copy(
-                sr.at[step, b, pl.ds(0, fields), pl.ds(s * RIM, RIM)],
-                hr.at[step, b, pl.ds(0, fields), pl.ds(s * RIM, RIM)],
-                row_ss.at[step, s, b], row_rs.at[step, s, b],
-                device_id=device(1 - 2 * s, 0), device_id_type=MESH,
-            )
-            for s in range(2)
-        ]
-        cols = [
-            pltpu.make_async_remote_copy(
-                sc.at[step, b, pl.ds(s * 8, 8)],
-                hc.at[step, b, pl.ds(s * 8, 8)],
-                col_ss.at[step, s, b], col_rs.at[step, s, b],
-                device_id=device(0, 1 - 2 * s), device_id_type=MESH,
-            )
-            for s in range(2)
-        ]
-        return rows + cols
-
-    for copy in depth_copies():
-        copy.start()
     for copy in near_copies(pk_s, pk_r, pk_ss, pk_rs, lambda k, di, dj: k):
         copy.start()
-
-    dep = depth[...]
-
-    def pack(step, b, row_fields, col_fields):
-        for f, source in enumerate(row_fields):
-            sr[step, b, f] = nn(c_sel[...], fld[source, b]).astype(BF16)
-        cols = nt(c_selc[0], fld[col_fields[0], b])
-        for f in range(1, len(col_fields)):
-            cols = cols + nt(c_selc[f], fld[col_fields[f], b])
-        sc[step, b] = cols
-        for copy in rim_copies(step, b, len(row_fields)):
-            copy.start()
-
-    def fill(idx, carry):
-        b = lax.rem(idx + 1, nb)
-        pltpu.make_async_copy(tracers.at[:, pl.ds(0, zb)], q.at[:, b], s_tr.at[b]).wait()
-        pltpu.make_async_copy(courant.at[:, pl.ds(0, zb)], cour.at[:, b], s_co.at[b]).wait()
-
-        def level(k, carry):
-            rows = pl.ds(pl.multiple_of(k * oy, oy), oy)
-            for t in range(ntr):
-                fld[t, b, rows, :] = q[t, b, k].astype(BF16)
-            wet = (b * zb + k) < dep
-            for a in range(2):
-                fld[ntr + a, b, rows, :] = jnp.where(wet, cour[a, b, k], 0.0).astype(BF16)
-            return carry
-
-        lax.fori_loop(0, zb, level, 0)
-        for f in range(ntr + 2):
-            fld[f, b, zb * oy :, :] = jnp.zeros((ROWS - zb * oy, ox), BF16)
-        pack(0, b, (0, 1, 2, 4), (0, 1, 2, 3))
-        return carry
-
-    lax.fori_loop(0, nb, fill, 0)
 
     for copy in depth_copies():
         copy.wait()
@@ -361,15 +396,23 @@
             for t in range(ntr):
                 moved = jnp.where(wet, q[t, b, k], 0.0)
                 moved = moved - (c0 * ux[t, rows, 0:ox] - c1 * ux[t, rows, ox : 2 * ox])
-                mv[t, k] = moved - (c2 * uy[t, rows, :] - c3 * uy[t, later, :])
+                moved = moved - (c2 * uy[t, rows, :] - c3 * uy[t, later, :])
+                mv[t, k] = moved.astype(BF16)
             return carry
 
         lax.fori_loop(0, zb, level, 0)
 
         @pl.when(b == 0)
         def _():
+            rows, later = pl.ds(0, oy), pl.ds(ROWS, oy)
+            wet = dep > 0
             for t in range(ntr):
-                mv[t, 0] = mv[t, 0] + jnp.where(dep > 0, forc[t], 0.0)
+                moved = jnp.where(wet, q[t, 0, 0] + forc[t], 0.0)
+                moved = moved - (
+                    coef[0, 0, 0] * ux[t, rows, 0:ox] - coef[1, 0, 0] * ux[t, rows, ox : 2 * ox]
+                )
+                moved = moved - (coef[2, 0, 0] * uy[t, rows, :] - coef[3, 0, 0] * uy[t, later, :])
+                mv[t, 0] = moved.astype(BF16)
 
     def mixing(b, keep):
         groups = zb // RGROUP
@@ -378,21 +421,27 @@
             lanes = pl.ds(pl.multiple_of((idx // groups) * LANES, LANES), LANES)
             first = lax.rem(idx, groups) * RGROUP
             acc = [[None] * ntr for _ in range(RGROUP)]
-            for c in range(zb):
-                moved = [mv[t, c, :, lanes] for t in range(ntr)]
+            for c0 in range(0, zb, CGROUP):
                 for r in range(RGROUP):
-                    weight = mixv[b, first + r, c, :, lanes].astype(F32)
+                    sums = [None] * ntr
+                    for c in range(c0, c0 + CGROUP):
+                        weight = mixv[b, first + r, c, :, lanes]
+                        for t in range(ntr):
+                            term = weight * mv[t, c, :, lanes]
+                            sums[t] = term if c == c0 else sums[t] + term
                     for t in range(ntr):
-                        term = weight * moved[t]
-                        acc[r][t] = term if c == 0 else acc[r][t] + term
+                        wide = sums[t].astype(F32)
+                        acc[r][t] = wide if c0 == 0 else acc[r][t] + wide
             for r in range(RGROUP):
                 k = first + r
                 wet = (b * zb + k) < depth[:, lanes]
                 for t in range(ntr):
                     value = jnp.where(wet, acc[r][t], 0.0)
-                    q[t, b, k, :, lanes] = value
                     if keep:
+                        q[t, b, k, :, lanes] = value
                         fld[t, b, pl.ds(pl.multiple_of(k * oy, oy), oy), lanes] = value.astype(BF16)
+                    else:
+                        out[t, b * zb + k, :, lanes] = value
             return carry
 
         lax.fori_loop(0, groups * (ox // LANES), part, 0)
@@ -432,7 +481,7 @@
 
     def give_back():
         pltpu.make_async_copy(to_atmos, toa, s_toa).wait()
-        surface = q[0, 0, 0].astype(BF16)
+        surface = out[0, 0].astype(BF16)
         y = iota((oy, slots * oy), 0)
         x = iota((oy, slots * oy), 1)
         diagonal = (x & 15) == y
@@ -459,6 +508,7 @@
         pltpu.make_async_copy(mix.at[0], mixv.at[b], s_mix.at[b]).wait()
         mixing(b, True)
         pack(1, b, (0, 1, 2), (0, 1, 2))
+        send(1, b, 3)
         return carry
 
     lax.fori_loop(0, nb, first_step, 0)
@@ -468,7 +518,6 @@
         wait_rims(1, b, 3)
         advect(1, b)
         mixing(b, False)
-        pltpu.make_async_copy(q.at[:, b], out.at[:, pl.ds(b * zb, zb)], s_out.at[b]).start()
 
         @pl.when(b == 0)
         def _():
@@ -493,8 +542,6 @@
     landed = nt(high, oh[...]) + nt(low, oh[...])
     for r in range(surf_out.shape[0]):
         surf_out[r : r + 1, :] = landed[0:1, r * LANES : (r + 1) * LANES]
-    for b in range(nb):
-        pltpu.make_async_copy(q.at[:, b], out.at[:, pl.ds(b * zb, zb)], s_out.at[b]).wait()
 
 
 def body(
@@ -517,9 +564,8 @@
     peers, slots = to_ocean.shape[:2]
     cells = atm_flux.shape[1] * atm_flux.shape[2]
     near = len(NEAR)
-    anywhere = pl.BlockSpec(memory_space=pl.ANY)
+    hbm = pl.BlockSpec(memory_space=pltpu.HBM)
     vmem = pl.BlockSpec(memory_space=pltpu.VMEM)
-    smem = pl.BlockSpec(memory_space=pltpu.SMEM)
     dma = pltpu.SemaphoreType.DMA
     scratch = [
         pltpu.VMEM((ntr, nb, zb, oy, ox), F32),
@@ -535,7 +581,7 @@
         pltpu.VMEM((4, nb, zb, oy, ox), F32),
         pltpu.VMEM((ntr, ROWS, 2 * ox), F32),
         pltpu.VMEM((ntr, 2 * ROWS, ox), F32),
-        pltpu.VMEM((ntr, zb, oy, ox), F32),
+        pltpu.VMEM((ntr, zb, oy, ox), BF16),
         pltpu.VMEM((ntr, oy, ox), F32),
         pltpu.VMEM((4, oy, ox), I32),
         pltpu.VMEM((2, 8, ox), I32),
@@ -557,12 +603,18 @@
         pltpu.VMEM((near, 8, slots), F32),
         pltpu.VMEM((peers, 8, slots), F32),
         pltpu.VMEM((near, 8, slots), F32),
+        pltpu.VMEM((oy, ox), I32),
+        pltpu.VMEM(atm_flux.shape, BF16),
+        pltpu.VMEM(slot_cell.shape, I32),
+        pltpu.SMEM(peer_list.shape, I32),
+        pltpu.SMEM(peer_count.shape, I32),
+        pltpu.SMEM(send_count.shape, I32),
+        dma((6,)),
         dma((nb,)),
         dma((nb,)),
         dma((nb,)),
         dma,
         dma,
-        dma((nb,)),
         dma((SUBSTEPS, 2, nb)),
         dma((SUBSTEPS, 2, nb)),
         dma((SUBSTEPS, 2, nb)),
@@ -577,14 +629,14 @@
     return pl.pallas_call(
         functools.partial(kernel, nty, ntx),
         out_shape=(
-            jax.ShapeDtypeStruct(tracers.shape, F32),
-            jax.ShapeDtypeStruct(atm_flux.shape[1:], F32),
+            pltpu.VMEM(tracers.shape, F32),
+            pltpu.VMEM(atm_flux.shape[1:], F32),
         ),
-        in_specs=[anywhere] * 5 + [vmem] * 3 + [smem] * 3,
-        out_specs=(anywhere, vmem),
+        in_specs=[hbm] * 11,
+        out_specs=(vmem, vmem),
         scratch_shapes=scratch,
         compiler_params=pltpu.CompilerParams(
-            collective_id=0, has_side_effects=True, vmem_limit_bytes=56 * 1024 * 1024
+            collective_id=0, has_side_effects=True, vmem_limit_bytes=62464 * 1024
         ),
         cost_estimate=pl.CostEstimate(flops=10**9, bytes_accessed=26 * 10**6, transcendentals=0),
         name="interval",

time: 55.2 us -> 51.6 us (0.935)
  local copies, waits for them, and re-layouts: 4.29 us -> 2.18 us
  Pallas kernels: 50.1 us -> 48.6 us
    unnamed x4 -> x2, local copies, waits for them, and re-layouts: 4.29 us -> 2.18 us
    pallas_call x1, Pallas kernels: 50.1 us -> 48.6 us  [body(): pl.pallas_call(functools.partial(kernel, nty, ntx), out_shape=(pltpu.VMEM...]
where the time goes in v1:
time: 51.6 us; the launch traced here: 51.4 us
  Pallas kernels  48.6 us (94%)
  local copies, waits for them, and re-layouts  2.18 us (4%)
  between operations  0.64 us (1%)
    pallas_call x1, Pallas kernels, body(): pl.pallas_call(functools.partial(kernel, nty, ntx), out_shape=(pltpu.VMEM...  48.6 us
    unnamed x2, local copies, waits for them, and re-layouts  2.18 us

profile of v1, /device:TPU:0, one launch (start us, length us, event | category | flops | bytes accessed | tf_op | source)
XLA Modules:
  0.0 51.4 jit_solution(9123319730847563859)
XLA Ops:
  0.6 48.6 %interval.1 = (f32[3,60,16,256]{3,2,1,0:T(8,128)S(1)}, f32[4,128]{1,0:T(4,128)S(1)}) custom-call(f32[3,60,16,256]{3,2,1,0:T(8,128)} %tracers.1, f32[2,60,16,256]{3,2,1,0:T(8,128)} %courant.1, bf16[4,15,15,16,256]{4,3,2,1,0:T(8,128)(2,1)} %mix.1, bf16[5,128,16,256]{3,2,1,0:T(8,128)(2,1)} %to_ocean.1, bf16[5,128,16,256]{3,2,1,0:T(8,128)(2,1)} %to_atmos.1, ...), custom_call_target="tpu_custom_call" | custom-call | flops 1000000000 | bytes 26000000 | tf_op jit(solution)/shard_map/interval/pallas_call | solution.py:629
  49.2 1.6 %copy.15 = f32[3,60,16,256]{3,2,1,0:T(8,128)} copy(f32[3,60,16,256]{3,2,1,0:T(8,128)S(1)} %get-tuple-element.2) | data formatting | bytes 5898240
  50.8 0.6 %copy.16 = f32[4,128]{1,0:T(4,128)} copy(f32[4,128]{1,0:T(4,128)S(1)} %get-tuple-element.3) | data formatting | bytes 4096

commit v2 on v1

--- a/solution.py
+++ b/solution.py
@@ -16,7 +16,8 @@
 RIM = 32
 ROWS = 256
 RGROUP = 5
-CGROUP = 5
+PAD = 32
+TOP = 8
 NEAR = tuple((di, dj) for di in (-1, 0, 1) for dj in (-1, 0, 1))
 
 
@@ -56,8 +57,8 @@
     send_count_in,
     out,
     surf_out,
-    q,
-    cour,
+    qs,
+    cx,
     mixv,
     toc,
     toa,
@@ -68,7 +69,7 @@
     hc,
     coef,
     ux,
-    uy,
+    tmp,
     mv,
     forc,
     depx,
@@ -78,13 +79,10 @@
     c_xh,
     c_xs,
     c_xsh,
-    c_y,
-    c_yh,
-    c_ys,
-    c_ysh,
     c_sel,
     c_selc,
     c_e,
+    c_et,
     oh,
     flat,
     pk_s,
@@ -99,7 +97,8 @@
     send_count,
     s_in,
     s_tr,
-    s_co,
+    s_cx,
+    s_cy,
     s_mix,
     s_toc,
     s_toa,
@@ -114,7 +113,10 @@
     rt_ss,
     rt_rs,
 ):
-    ntr, nb, zb, oy, ox = q.shape
+    nb, zb = mix.shape[:2]
+    ntr, _, oy, ox = tracers.shape
+    halves = ox // LANES
+    own = slice(TOP, TOP + oy)
     peers, slots = to_ocean.shape[0], to_ocean.shape[1]
     i = lax.axis_index("ty")
     j = lax.axis_index("tx")
@@ -142,16 +144,32 @@
     ]
     small[0].start()
     order = tuple((n + 1) % nb for n in range(nb))
-    loads = {}
+
+    def loads(b, first):
+        made = []
+        for h in range(halves):
+            lanes = pl.ds(h * LANES, LANES)
+            levels = pl.ds(first, zb)
+            made += [
+                pltpu.make_async_copy(
+                    tracers.at[:, levels, :, lanes],
+                    qs.at[pl.ds(0, ntr), b, :, h, pl.ds(TOP, oy)],
+                    s_tr.at[h, b],
+                ),
+                pltpu.make_async_copy(
+                    courant.at[0, levels, :, lanes], cx.at[b, :, h], s_cx.at[h, b]
+                ),
+                pltpu.make_async_copy(
+                    courant.at[1, levels, :, lanes],
+                    qs.at[ntr, b, :, h, pl.ds(TOP, oy)],
+                    s_cy.at[h, b],
+                ),
+            ]
+        return made
+
     for b in order:
-        loads["tr", b] = pltpu.make_async_copy(
-            tracers.at[:, pl.ds(b * zb, zb)], q.at[:, b], s_tr.at[b]
-        )
-        loads["co", b] = pltpu.make_async_copy(
-            courant.at[:, pl.ds(b * zb, zb)], cour.at[:, b], s_co.at[b]
-        )
-        loads["tr", b].start()
-        loads["co", b].start()
+        for copy in loads(b, b * zb):
+            copy.start()
     for copy in small[1:]:
         copy.start()
     for b in order[:-1]:
@@ -246,19 +264,16 @@
             copy.start()
 
     def fill(b):
-        pltpu.make_async_copy(tracers.at[:, pl.ds(0, zb)], q.at[:, b], s_tr.at[b]).wait()
-        pltpu.make_async_copy(courant.at[:, pl.ds(0, zb)], cour.at[:, b], s_co.at[b]).wait()
-
-        def level(k, carry):
-            rows = pl.ds(pl.multiple_of(k * oy, oy), oy)
-            for t in range(ntr):
-                fld[t, b, rows, :] = q[t, b, k].astype(BF16)
-            wet = (b * zb + k) < dep
-            for a in range(2):
-                fld[ntr + a, b, rows, :] = jnp.where(wet, cour[a, b, k], 0.0).astype(BF16)
-            return carry
-
-        lax.fori_loop(0, zb, level, 0)
+        for copy in loads(b, 0):
+            copy.wait()
+        for h in range(halves):
+            lanes = slice(h * LANES, (h + 1) * LANES)
+            for f in range(ntr + 2):
+                if f == ntr:
+                    value = cx[b, :, h]
+                else:
+                    value = qs[min(f, ntr), b, :, h, own, :]
+                fld[f, b, 0 : zb * oy, lanes] = value.reshape(zb * oy, LANES).astype(BF16)
         for f in range(ntr + 2):
             fld[f, b, zb * oy :, :] = jnp.zeros((ROWS - zb * oy, ox), BF16)
         pack(0, b, (0, 1, 2, 4), (0, 1, 2, 3))
@@ -293,28 +308,12 @@
         else:
             hit = mine & (at - x == jnp.where(n < ox, 1, 0))
             c_xsh[...] = jnp.where(hit, 1.0, 0.0).astype(BF16)
-    m = iota((2 * ROWS, ROWS), 0)
-    n = iota((2 * ROWS, ROWS), 1)
-    mm = jnp.where(m < ROWS, m, m - ROWS)
-    y = jnp.where(m < ROWS, mm & 15, (mm & 15) - 1)
-    d = (n & 15) - y
-    same = (mm >> 4) == (n >> 4)
-    c_y[...] = jnp.where(same, stencil(d), 0.0).astype(BF16)
-    hit = same & (d == jnp.where(m < ROWS, 1, 0))
-    c_ys[...] = jnp.where(hit, 1.0, 0.0).astype(BF16)
-    m = iota((2 * ROWS, 2 * RIM), 0)
-    n = iota((2 * ROWS, 2 * RIM), 1)
-    mm = jnp.where(m < ROWS, m, m - ROWS)
-    y = jnp.where(m < ROWS, mm & 15, (mm & 15) - 1)
-    nn_ = jnp.where(n < RIM, n, n - RIM)
-    d = jnp.where(n < RIM, -2 + (nn_ & 1), oy + (nn_ & 1)) - y
-    same = (mm >> 4) == (nn_ >> 1)
-    c_yh[...] = jnp.where(same, stencil(d), 0.0).astype(BF16)
-    hit = same & (d == jnp.where(m < ROWS, 1, 0))
-    c_ysh[...] = jnp.where(hit, 1.0, 0.0).astype(BF16)
     r = iota((slots, slots * oy), 0)
     n = iota((slots, slots * oy), 1)
     c_e[...] = jnp.where((n >> 4) == r, 1.0, 0.0).astype(BF16)
+    r = iota((slots * oy, slots), 0)
+    n = iota((slots * oy, slots), 1)
+    c_et[...] = jnp.where((r >> 4) == n, 1.0, 0.0).astype(BF16)
 
     for copy in small[1:]:
         copy.wait()
@@ -355,96 +354,89 @@
         for copy in rim_copies(step, b, fields):
             copy.wait()
 
+    def place(step, b, fields):
+        for f in range(fields):
+            for h in range(halves):
+                tmp[f, h] = hr[step, b, f, :, h * LANES : (h + 1) * LANES].astype(F32)
+        for f in range(fields):
+            for h in range(halves):
+                for k in range(zb):
+                    qs[f, b, k, h, TOP - 2 : TOP, :] = tmp[f, h, 2 * k : 2 * k + 2, :]
+                    qs[f, b, k, h, TOP + oy : TOP + oy + 2, :] = tmp[
+                        f, h, RIM + 2 * k : RIM + 2 * k + 2, :
+                    ]
+
     def faces(b):
         ux[0] = nn(fld[ntr, b], c_xs[...]) + tn(hc[0, b].astype(BF16), c_xsh[...])
-        uy[0] = nn(c_ys[...], fld[ntr + 1, b]) + nn(c_ysh[...], hr[0, b, ntr])
-
-        def level(k, carry):
-            rows = pl.ds(pl.multiple_of(k * oy, oy), oy)
-            later = pl.ds(pl.multiple_of(ROWS + k * oy, oy), oy)
+        for k in range(zb):
             at = b * zb + k
-            wet = at < dep
-            own = jnp.where(wet, cour[0, b, k] * (1.0 / 24.0), 0.0)
-            coef[0, b, k] = jnp.where(at < depx[0], own, 0.0) + jnp.where(
-                wet, ux[0, rows, 0:ox] * (1.0 / 24.0), 0.0
-            )
-            coef[1, b, k] = jnp.where(at < depx[1], own, 0.0) + jnp.where(
-                wet, ux[0, rows, ox : 2 * ox] * (1.0 / 24.0), 0.0
-            )
-            own = jnp.where(wet, cour[1, b, k] * (1.0 / 24.0), 0.0)
-            coef[2, b, k] = jnp.where(at < depx[2], own, 0.0) + jnp.where(
-                wet, uy[0, rows, :] * (1.0 / 24.0), 0.0
-            )
-            coef[3, b, k] = jnp.where(at < depx[3], own, 0.0) + jnp.where(
-                wet, uy[0, later, :] * (1.0 / 24.0), 0.0
-            )
-            return carry
-
-        lax.fori_loop(0, zb, level, 0)
+            rows = slice(k * oy, (k + 1) * oy)
+            for h in range(halves):
+                lanes = slice(h * LANES, (h + 1) * LANES)
+                wet = at < depth[:, lanes]
+                near_wet = [wet & (at < depx[a, :, lanes]) for a in range(4)]
+                x0 = cx[b, k, h]
+                y0 = qs[ntr, b, k, h, own, :]
+                others = (
+                    ux[0, rows, lanes],
+                    ux[0, rows, ox + h * LANES : ox + (h + 1) * LANES],
+                    qs[ntr, b, k, h, TOP + 1 : TOP + 1 + oy, :],
+                    qs[ntr, b, k, h, TOP - 1 : TOP - 1 + oy, :],
+                )
+                for a in range(4):
+                    mean = ((x0, y0)[a // 2] + others[a]) * (1.0 / 24.0)
+                    coef[a, b, k, h] = jnp.where(near_wet[a], mean, 0.0)
 
     def advect(step, b):
         halo = hc[step, b].astype(BF16)
         for t in range(ntr):
             ux[t] = nn(fld[t, b], c_x[...]) + tn(halo, c_xh[t])
-            uy[t] = nn(c_y[...], fld[t, b]) + nn(c_yh[...], hr[step, b, t])
-
-        def level(k, carry):
-            rows = pl.ds(pl.multiple_of(k * oy, oy), oy)
-            later = pl.ds(pl.multiple_of(ROWS + k * oy, oy), oy)
-            wet = (b * zb + k) < dep
-            c0, c1, c2, c3 = (coef[a, b, k] for a in range(4))
-            for t in range(ntr):
-                moved = jnp.where(wet, q[t, b, k], 0.0)
-                moved = moved - (c0 * ux[t, rows, 0:ox] - c1 * ux[t, rows, ox : 2 * ox])
-                moved = moved - (c2 * uy[t, rows, :] - c3 * uy[t, later, :])
-                mv[t, k] = moved.astype(BF16)
-            return carry
-
-        lax.fori_loop(0, zb, level, 0)
+        for k in range(zb):
+            rows = slice(k * oy, (k + 1) * oy)
+            for h in range(halves):
+                lanes = slice(h * LANES, (h + 1) * LANES)
+                c0, c1, c2, c3 = (coef[a, b, k, h] for a in range(4))
+                for t in range(ntr):
+                    m2, m1, q0, p1, p2 = (
+                        qs[t, b, k, h, TOP + o : TOP + o + oy, :] for o in (-2, -1, 0, 1, 2)
+                    )
+                    east = c0 * ux[t, rows, lanes]
+                    west = c1 * ux[t, rows, ox + h * LANES : ox + (h + 1) * LANES]
+                    north = c2 * (7.0 * (q0 + p1) - (m1 + p2))
+                    south = c3 * (7.0 * (m1 + q0) - (m2 + p1))
+                    if step == 0:
+                        q0 = jnp.where((b * zb + k) < depth[:, lanes], q0, 0.0)
+                    mv[t, k, h] = q0 - (east - west) - (north - south)
 
         @pl.when(b == 0)
         def _():
-            rows, later = pl.ds(0, oy), pl.ds(ROWS, oy)
-            wet = dep > 0
             for t in range(ntr):
-                moved = jnp.where(wet, q[t, 0, 0] + forc[t], 0.0)
-                moved = moved - (
-                    coef[0, 0, 0] * ux[t, rows, 0:ox] - coef[1, 0, 0] * ux[t, rows, ox : 2 * ox]
-                )
-                moved = moved - (coef[2, 0, 0] * uy[t, rows, :] - coef[3, 0, 0] * uy[t, later, :])
-                mv[t, 0] = moved.astype(BF16)
+                for h in range(halves):
+                    lanes = slice(h * LANES, (h + 1) * LANES)
+                    mv[t, 0, h] = mv[t, 0, h] + jnp.where(depth[:, lanes] > 0, forc[t, :, lanes], 0.0)
 
     def mixing(b, keep):
-        groups = zb // RGROUP
-
-        def part(idx, carry):
-            lanes = pl.ds(pl.multiple_of((idx // groups) * LANES, LANES), LANES)
-            first = lax.rem(idx, groups) * RGROUP
-            acc = [[None] * ntr for _ in range(RGROUP)]
-            for c0 in range(0, zb, CGROUP):
+        for h in range(halves):
+            lanes = slice(h * LANES, (h + 1) * LANES)
+            for first in range(0, zb, RGROUP):
+                acc = [[None] * ntr for _ in range(RGROUP)]
+                for c in range(zb):
+                    moved = [mv[t, c, h] for t in range(ntr)]
+                    for r in range(RGROUP):
+                        weight = mixv[b, first + r, c, :, lanes].astype(F32)
+                        for t in range(ntr):
+                            term = weight * moved[t]
+                            acc[r][t] = term if c == 0 else acc[r][t] + term
                 for r in range(RGROUP):
-                    sums = [None] * ntr
-                    for c in range(c0, c0 + CGROUP):
-                        weight = mixv[b, first + r, c, :, lanes]
-                        for t in range(ntr):
-                            term = weight * mv[t, c, :, lanes]
-                            sums[t] = term if c == c0 else sums[t] + term
+                    k = first + r
+                    wet = (b * zb + k) < depth[:, lanes]
                     for t in range(ntr):
-                        wide = sums[t].astype(F32)
-                        acc[r][t] = wide if c0 == 0 else acc[r][t] + wide
-            for r in range(RGROUP):
-                k = first + r
-                wet = (b * zb + k) < depth[:, lanes]
-                for t in range(ntr):
-                    value = jnp.where(wet, acc[r][t], 0.0)
-                    if keep:
-                        q[t, b, k, :, lanes] = value
-                        fld[t, b, pl.ds(pl.multiple_of(k * oy, oy), oy), lanes] = value.astype(BF16)
-                    else:
-                        out[t, b * zb + k, :, lanes] = value
-            return carry
-
-        lax.fori_loop(0, groups * (ox // LANES), part, 0)
+                        value = jnp.where(wet, acc[r][t], 0.0)
+                        if keep:
+                            qs[t, b, k, h, own, :] = value
+                            fld[t, b, k * oy : (k + 1) * oy, lanes] = value.astype(BF16)
+                        else:
+                            out[t, b * zb + k, :, lanes] = value
 
     def force():
         for copy in near_copies(pk_s, pk_r, pk_ss, pk_rs, lambda k, di, dj: k):
@@ -464,11 +456,14 @@
         x = iota((oy, slots * oy), 1)
         diagonal = (x & 15) == y
         total = jnp.zeros((ntr * oy, ox), F32)
+        live = [jnp.where(slot < peer_count[0, 0, p], chosen[p], 0.0) for p in range(peers)]
+        spread = nn(jnp.concatenate(live, axis=0).astype(BF16), c_e[...])
         for p in range(peers):
-            live = jnp.where(slot < peer_count[0, 0, p], chosen[p], 0.0).astype(BF16)
-            spread = nn(live, c_e[...])
             left = jnp.concatenate(
-                [jnp.where(diagonal, spread[c : c + 1, :], 0.0).astype(BF16) for c in range(ntr)],
+                [
+                    jnp.where(diagonal, spread[8 * p + c : 8 * p + c + 1, :], 0.0).astype(BF16)
+                    for c in range(ntr)
+                ],
                 axis=0,
             )
             total = total + nn(left, toc[p].reshape(slots * oy, ox))
@@ -485,19 +480,25 @@
         y = iota((oy, slots * oy), 0)
         x = iota((oy, slots * oy), 1)
         diagonal = (x & 15) == y
+        rows = []
         for p in range(peers):
             sums = nt(surface, toa[p].reshape(slots * oy, ox))
-            sums = jnp.where(diagonal, sums, 0.0)
-            high = sums.astype(BF16)
-            low = (sums - high.astype(F32)).astype(BF16)
-            both = nt(high, c_e[...]) + nt(low, c_e[...])
-            rt_s[p] = jnp.broadcast_to(jnp.sum(both, axis=0, keepdims=True), (8, slots))
+            rows.append(jnp.sum(jnp.where(diagonal, sums, 0.0), axis=0, keepdims=True))
+        rows.append(jnp.zeros((8 - peers, slots * oy), F32))
+        sums = jnp.concatenate(rows, axis=0)
+        high = sums.astype(BF16)
+        low = (sums - high.astype(F32)).astype(BF16)
+        both = nn(jnp.concatenate([high, low], axis=0), c_et[...])
+        both = both[0:8] + both[8:16]
+        for p in range(peers):
+            rt_s[p] = jnp.broadcast_to(both[p : p + 1], (8, slots))
         for copy in ret_copies():
             copy.start()
 
     def first_step(idx, carry):
         b = lax.rem(idx + 1, nb)
         wait_rims(0, b, 4)
+        place(0, b, ntr + 1)
         faces(b)
 
         @pl.when(b == 0)
@@ -516,6 +517,7 @@
     def second_step(idx, carry):
         b = jnp.where(idx < 2, 1 - idx, idx)
         wait_rims(1, b, 3)
+        place(1, b, ntr)
         advect(1, b)
         mixing(b, False)
 
@@ -568,8 +570,8 @@
     vmem = pl.BlockSpec(memory_space=pltpu.VMEM)
     dma = pltpu.SemaphoreType.DMA
     scratch = [
-        pltpu.VMEM((ntr, nb, zb, oy, ox), F32),
-        pltpu.VMEM((2, nb, zb, oy, ox), F32),
+        pltpu.VMEM((ntr + 1, nb, zb, ox // LANES, PAD, LANES), F32),
+        pltpu.VMEM((nb, zb, ox // LANES, oy, LANES), F32),
         pltpu.VMEM(mix_inverse.shape, BF16),
         pltpu.VMEM(to_ocean.shape, BF16),
         pltpu.VMEM(to_atmos.shape, BF16),
@@ -578,10 +580,10 @@
         pltpu.VMEM((SUBSTEPS, nb, 4, 2 * RIM, ox), BF16),
         pltpu.VMEM((SUBSTEPS, nb, 16, ox), F32),
         pltpu.VMEM((SUBSTEPS, nb, 16, ox), F32),
-        pltpu.VMEM((4, nb, zb, oy, ox), F32),
+        pltpu.VMEM((4, nb, zb, ox // LANES, oy, LANES), F32),
         pltpu.VMEM((ntr, ROWS, 2 * ox), F32),
-        pltpu.VMEM((ntr, 2 * ROWS, ox), F32),
-        pltpu.VMEM((ntr, zb, oy, ox), BF16),
+        pltpu.VMEM((ntr + 1, ox // LANES, 2 * RIM, LANES), F32),
+        pltpu.VMEM((ntr, zb, ox // LANES, oy, LANES), F32),
         pltpu.VMEM((ntr, oy, ox), F32),
         pltpu.VMEM((4, oy, ox), I32),
         pltpu.VMEM((2, 8, ox), I32),
@@ -590,13 +592,10 @@
         pltpu.VMEM((3, 16, 2 * ox), BF16),
         pltpu.VMEM((ox, 2 * ox), BF16),
         pltpu.VMEM((16, 2 * ox), BF16),
-        pltpu.VMEM((2 * ROWS, ROWS), BF16),
-        pltpu.VMEM((2 * ROWS, 2 * RIM), BF16),
-        pltpu.VMEM((2 * ROWS, ROWS), BF16),
-        pltpu.VMEM((2 * ROWS, 2 * RIM), BF16),
         pltpu.VMEM((2 * RIM, ROWS), BF16),
         pltpu.VMEM((4, 16, ox), BF16),
         pltpu.VMEM((slots, slots * oy), BF16),
+        pltpu.VMEM((slots * oy, slots), BF16),
         pltpu.VMEM((cells, near * slots), BF16),
         pltpu.VMEM((8, cells), F32),
         pltpu.VMEM((near, 8, slots), F32),
@@ -610,8 +609,9 @@
         pltpu.SMEM(peer_count.shape, I32),
         pltpu.SMEM(send_count.shape, I32),
         dma((6,)),
-        dma((nb,)),
-        dma((nb,)),
+        dma((ox // LANES, nb)),
+        dma((ox // LANES, nb)),
+        dma((ox // LANES, nb)),
         dma((nb,)),
         dma,
         dma,

time: 51.6 us -> 42.4 us (0.82)
  Pallas kernels: 48.6 us -> 39.4 us
    pallas_call x1, Pallas kernels: 48.6 us -> 39.4 us  [body(): pl.pallas_call(functools.partial(kernel, nty, ntx), out_shape=(pltpu.VMEM...]
where the time goes in v2:
time: 42.4 us; the launch traced here: 42.3 us
  Pallas kernels  39.4 us (93%)
  local copies, waits for them, and re-layouts  2.18 us (5%)
  between operations  0.64 us (2%)
    pallas_call x1, Pallas kernels, body(): pl.pallas_call(functools.partial(kernel, nty, ntx), out_shape=(pltpu.VMEM...  39.4 us
    unnamed x2, local copies, waits for them, and re-layouts  2.18 us

profile of v2, /device:TPU:0, one launch (start us, length us, event | category | flops | bytes accessed | tf_op | source)
XLA Modules:
  0.0 42.3 jit_solution(8661483939860356359)
XLA Ops:
  0.6 39.4 %interval.1 = (f32[3,60,16,256]{3,2,1,0:T(8,128)S(1)}, f32[4,128]{1,0:T(4,128)S(1)}) custom-call(f32[3,60,16,256]{3,2,1,0:T(8,128)} %tracers.1, f32[2,60,16,256]{3,2,1,0:T(8,128)} %courant.1, bf16[4,15,15,16,256]{4,3,2,1,0:T(8,128)(2,1)} %mix.1, bf16[5,128,16,256]{3,2,1,0:T(8,128)(2,1)} %to_ocean.1, bf16[5,128,16,256]{3,2,1,0:T(8,128)(2,1)} %to_atmos.1, ...), custom_call_target="tpu_custom_call" | custom-call | flops 1000000000 | bytes 26000000 | tf_op jit(solution)/shard_map/interval/pallas_call | solution.py:629
  40.1 1.6 %copy.15 = f32[3,60,16,256]{3,2,1,0:T(8,128)} copy(f32[3,60,16,256]{3,2,1,0:T(8,128)S(1)} %get-tuple-element.2) | data formatting | bytes 5898240
  41.7 0.6 %copy.16 = f32[4,128]{1,0:T(4,128)} copy(f32[4,128]{1,0:T(4,128)S(1)} %get-tuple-element.3) | data formatting | bytes 4096

commit v3 on v2

--- a/solution.py
+++ b/solution.py
@@ -79,7 +79,6 @@
     c_xh,
     c_xs,
     c_xsh,
-    c_sel,
     c_selc,
     c_e,
     c_et,
@@ -178,23 +177,25 @@
     pltpu.make_async_copy(mix.at[order[-1]], mixv.at[order[-1]], s_mix.at[order[-1]]).start()
     pltpu.make_async_copy(to_atmos, toa, s_toa).start()
 
-    m = iota((2 * RIM, ROWS), 0)
-    n = iota((2 * RIM, ROWS), 1)
-    mm = jnp.where(m < RIM, m, m - RIM)
-    y = jnp.where(m < RIM, oy - 2 + (mm & 1), mm & 1)
-    open_down = jnp.where(i == nty - 1, 0.0, 1.0)
-    open_up = jnp.where(i == 0, 0.0, 1.0)
-    hit = ((mm >> 1) == (n >> 4)) & ((n & 15) == y)
-    c_sel[...] = jnp.where(hit, jnp.where(m < RIM, open_down, open_up), 0.0).astype(BF16)
     r = iota((16, ox), 0)
     n = iota((16, ox), 1)
-    open_right = jnp.where(j == ntx - 1, 0.0, 1.0)
-    open_left = jnp.where(j == 0, 0.0, 1.0)
     for f in range(4):
         at = jnp.where(r < 8, ox - 2 + r - 2 * f, r - 8 - 2 * f)
         mine = ((r & 7) >> 1) == f
         hit = mine & (at == n)
-        c_selc[f] = jnp.where(hit, jnp.where(r < 8, open_right, open_left), 0.0).astype(BF16)
+        c_selc[f] = jnp.where(hit, 1.0, 0.0).astype(BF16)
+    sends = (i < nty - 1, i > 0, j < ntx - 1, j > 0)
+    takes = (i > 0, i < nty - 1, j > 0, j < ntx - 1)
+
+    def start_all(copies):
+        for copy, mine in zip(copies, sends):
+            pl.when(mine)(copy.start)
+
+    def wait_all(copies):
+        for copy, mine, theirs in zip(copies, sends, takes):
+            pl.when(mine)(copy.wait_send)
+            pl.when(theirs)(copy.wait_recv)
+
     def depth_copies():
         return (
             pltpu.make_async_remote_copy(
@@ -252,36 +253,48 @@
     dep = depth[...]
 
     def pack(step, b, row_fields, col_fields):
-        for f, source in enumerate(row_fields):
-            sr[step, b, f] = nn(c_sel[...], fld[source, b]).astype(BF16)
-        cols = nt(c_selc[0], fld[col_fields[0], b])
-        for f in range(1, len(col_fields)):
-            cols = cols + nt(c_selc[f], fld[col_fields[f], b])
+        for f in range(row_fields):
+            for h in range(halves):
+                for k in range(zb):
+                    tmp[f, h, 2 * k : 2 * k + 2, :] = qs[f, b, k, h, TOP + oy - 2 : TOP + oy, :]
+                    tmp[f, h, RIM + 2 * k : RIM + 2 * k + 2, :] = qs[f, b, k, h, TOP : TOP + 2, :]
+                sr[step, b, f, :, h * LANES : (h + 1) * LANES] = tmp[f, h].astype(BF16)
+        cols = nt(c_selc[0], fld[0, b])
+        for f in range(1, col_fields):
+            cols = cols + nt(c_selc[f], fld[f, b])
         sc[step, b] = cols
 
     def send(step, b, fields):
-        for copy in rim_copies(step, b, fields):
-            copy.start()
+        start_all(rim_copies(step, b, fields))
 
     def fill(b):
         for copy in loads(b, 0):
             copy.wait()
         for h in range(halves):
             lanes = slice(h * LANES, (h + 1) * LANES)
-            for f in range(ntr + 2):
-                if f == ntr:
-                    value = cx[b, :, h]
-                else:
-                    value = qs[min(f, ntr), b, :, h, own, :]
+            for f in range(ntr + 1):
+                value = cx[b, :, h] if f == ntr else qs[f, b, :, h, own, :]
                 fld[f, b, 0 : zb * oy, lanes] = value.reshape(zb * oy, LANES).astype(BF16)
-        for f in range(ntr + 2):
+        for f in range(ntr + 1):
             fld[f, b, zb * oy :, :] = jnp.zeros((ROWS - zb * oy, ox), BF16)
-        pack(0, b, (0, 1, 2, 4), (0, 1, 2, 3))
-
+        pack(0, b, ntr + 1, ntr + 1)
+
+    tmp[...] = jnp.zeros_like(tmp)
     fill(order[0])
+
+    for s in range(2):
+        @pl.when(jnp.logical_not(takes[s]))
+        def _():
+            hr[:, :, :, s * RIM : (s + 1) * RIM, :] = jnp.zeros((SUBSTEPS, nb, 4, RIM, ox), BF16)
+            dr[s] = jnp.zeros((8, ox), I32)
+
+        @pl.when(jnp.logical_not(takes[2 + s]))
+        def _():
+            hc[:, :, s * 8 : (s + 1) * 8, :] = jnp.zeros((SUBSTEPS, nb, 8, ox), F32)
+            dc[s] = jnp.zeros((oy, LANES), I32)
+
     pl.semaphore_wait(barrier, len(NEAR) - 1)
-    for copy in depth_copies():
-        copy.start()
+    start_all(depth_copies())
     send(0, order[0], 4)
 
     def fill_and_send(idx, carry):
@@ -335,12 +348,8 @@
     for copy in near_copies(pk_s, pk_r, pk_ss, pk_rs, lambda k, di, dj: k):
         copy.start()
 
-    for copy in depth_copies():
-        copy.wait()
-    south = jnp.where(i == 0, 0, dr[0])
-    north = jnp.where(i == nty - 1, 0, dr[1])
-    west = jnp.where(j == 0, 0, dc[0])
-    east = jnp.where(j == ntx - 1, 0, dc[1])
+    wait_all(depth_copies())
+    south, north, west, east = dr[0], dr[1], dc[0], dc[1]
     wide = jnp.concatenate([dep, east], axis=1)
     depx[0] = pltpu.roll(wide, ox + LANES - 1, 1)[:, :ox]
     wide = jnp.concatenate([west, dep], axis=1)
@@ -351,8 +360,7 @@
     depx[3] = pltpu.roll(tall, 1, 0)[8:]
 
     def wait_rims(step, b, fields):
-        for copy in rim_copies(step, b, fields):
-            copy.wait()
+        wait_all(rim_copies(step, b, fields))
 
     def place(step, b, fields):
         for f in range(fields):
@@ -508,7 +516,7 @@
         advect(0, b)
         pltpu.make_async_copy(mix.at[0], mixv.at[b], s_mix.at[b]).wait()
         mixing(b, True)
-        pack(1, b, (0, 1, 2), (0, 1, 2))
+        pack(1, b, ntr, ntr)
         send(1, b, 3)
         return carry
 
@@ -575,7 +583,7 @@
         pltpu.VMEM(mix_inverse.shape, BF16),
         pltpu.VMEM(to_ocean.shape, BF16),
         pltpu.VMEM(to_atmos.shape, BF16),
-        pltpu.VMEM((ntr + 2, nb, ROWS, ox), BF16),
+        pltpu.VMEM((ntr + 1, nb, ROWS, ox), BF16),
         pltpu.VMEM((SUBSTEPS, nb, 4, 2 * RIM, ox), BF16),
         pltpu.VMEM((SUBSTEPS, nb, 4, 2 * RIM, ox), BF16),
         pltpu.VMEM((SUBSTEPS, nb, 16, ox), F32),
@@ -592,7 +600,6 @@
         pltpu.VMEM((3, 16, 2 * ox), BF16),
         pltpu.VMEM((ox, 2 * ox), BF16),
         pltpu.VMEM((16, 2 * ox), BF16),
-        pltpu.VMEM((2 * RIM, ROWS), BF16),
         pltpu.VMEM((4, 16, ox), BF16),
         pltpu.VMEM((slots, slots * oy), BF16),
         pltpu.VMEM((slots * oy, slots), BF16),

time: 42.4 us -> 38.8 us (0.915)
  Pallas kernels: 39.4 us -> 35.7 us
    pallas_call x1, Pallas kernels: 39.4 us -> 35.7 us  [body(): pl.pallas_call(functools.partial(kernel, nty, ntx), out_shape=(pltpu.VMEM...]
where the time goes in v3:
time: 38.8 us; the launch traced here: 38.5 us
  Pallas kernels  35.7 us (92%)
  local copies, waits for them, and re-layouts  2.18 us (6%)
  between operations  0.64 us (2%)
    pallas_call x1, Pallas kernels, body(): pl.pallas_call(functools.partial(kernel, nty, ntx), out_shape=(pltpu.VMEM...  35.7 us
    unnamed x2, local copies, waits for them, and re-layouts  2.18 us

profile of v3, /device:TPU:0, one launch (start us, length us, event | category | flops | bytes accessed | tf_op | source)
XLA Modules:
  0.0 38.5 jit_solution(9134628100666141944)
XLA Ops:
  0.6 35.7 %interval.1 = (f32[3,60,16,256]{3,2,1,0:T(8,128)S(1)}, f32[4,128]{1,0:T(4,128)S(1)}) custom-call(f32[3,60,16,256]{3,2,1,0:T(8,128)} %tracers.1, f32[2,60,16,256]{3,2,1,0:T(8,128)} %courant.1, bf16[4,15,15,16,256]{4,3,2,1,0:T(8,128)(2,1)} %mix.1, bf16[5,128,16,256]{3,2,1,0:T(8,128)(2,1)} %to_ocean.1, bf16[5,128,16,256]{3,2,1,0:T(8,128)(2,1)} %to_atmos.1, ...), custom_call_target="tpu_custom_call" | custom-call | flops 1000000000 | bytes 26000000 | tf_op jit(solution)/shard_map/interval/pallas_call | solution.py:636
  36.3 1.6 %copy.15 = f32[3,60,16,256]{3,2,1,0:T(8,128)} copy(f32[3,60,16,256]{3,2,1,0:T(8,128)S(1)} %get-tuple-element.2) | data formatting | bytes 5898240
  37.9 0.6 %copy.16 = f32[4,128]{1,0:T(4,128)} copy(f32[4,128]{1,0:T(4,128)S(1)} %get-tuple-element.3) | data formatting | bytes 4096

commit v4 on v3

--- a/solution.py
+++ b/solution.py
@@ -142,7 +142,7 @@
         )
     ]
     small[0].start()
-    order = tuple((n + 1) % nb for n in range(nb))
+    order = (1, 0) + tuple(range(2, nb))
 
     def loads(b, first):
         made = []
@@ -171,10 +171,10 @@
             copy.start()
     for copy in small[1:]:
         copy.start()
-    for b in order[:-1]:
+    pltpu.make_async_copy(mix.at[order[0]], mixv.at[order[0]], s_mix.at[order[0]]).start()
+    pltpu.make_async_copy(to_ocean, toc, s_toc).start()
+    for b in order[1:]:
         pltpu.make_async_copy(mix.at[b], mixv.at[b], s_mix.at[b]).start()
-    pltpu.make_async_copy(to_ocean, toc, s_toc).start()
-    pltpu.make_async_copy(mix.at[order[-1]], mixv.at[order[-1]], s_mix.at[order[-1]]).start()
     pltpu.make_async_copy(to_atmos, toa, s_toa).start()
 
     r = iota((16, ox), 0)
@@ -298,12 +298,32 @@
     send(0, order[0], 4)
 
     def fill_and_send(idx, carry):
-        b = lax.rem(idx + 1, nb)
+        b = jnp.where(idx < 2, 1 - idx, idx)
         fill(b)
         send(0, b, 4)
         return carry
 
     lax.fori_loop(1, nb, fill_and_send, 0)
+
+    for copy in small[1:]:
+        copy.wait()
+
+    cells = iota((oh.shape[0], slots), 0)
+    for k, (di, dj) in enumerate(NEAR):
+        ti, tj = device(di, dj)
+        row = slot_cell[0, 0, pl.ds(ti * ntx + tj, 1), :]
+        oh[:, k * slots : (k + 1) * slots] = jnp.where(cells == row, 1.0, 0.0).astype(BF16)
+    flux = atm[...].astype(F32)
+    flat[...] = jnp.zeros_like(flat)
+    for c in range(flux.shape[0]):
+        for r in range(flux.shape[1]):
+            flat[c : c + 1, r * LANES : (r + 1) * LANES] = flux[c, r : r + 1, :]
+    picks = nn(flat[...].astype(BF16), oh[...])
+    for k in range(len(NEAR)):
+        pk_s[k] = picks[:, k * slots : (k + 1) * slots]
+
+    for copy in near_copies(pk_s, pk_r, pk_ss, pk_rs, lambda k, di, dj: k):
+        copy.start()
 
     g = iota((ox, 2 * ox), 0)
     n = iota((ox, 2 * ox), 1)
@@ -327,26 +347,6 @@
     r = iota((slots * oy, slots), 0)
     n = iota((slots * oy, slots), 1)
     c_et[...] = jnp.where((r >> 4) == n, 1.0, 0.0).astype(BF16)
-
-    for copy in small[1:]:
-        copy.wait()
-
-    cells = iota((oh.shape[0], slots), 0)
-    for k, (di, dj) in enumerate(NEAR):
-        ti, tj = device(di, dj)
-        row = slot_cell[0, 0, pl.ds(ti * ntx + tj, 1), :]
-        oh[:, k * slots : (k + 1) * slots] = jnp.where(cells == row, 1.0, 0.0).astype(BF16)
-    flux = atm[...].astype(F32)
-    flat[...] = jnp.zeros_like(flat)
-    for c in range(flux.shape[0]):
-        for r in range(flux.shape[1]):
-            flat[c : c + 1, r * LANES : (r + 1) * LANES] = flux[c, r : r + 1, :]
-    picks = nn(flat[...].astype(BF16), oh[...])
-    for k in range(len(NEAR)):
-        pk_s[k] = picks[:, k * slots : (k + 1) * slots]
-
-    for copy in near_copies(pk_s, pk_r, pk_ss, pk_rs, lambda k, di, dj: k):
-        copy.start()
 
     wait_all(depth_copies())
     south, north, west, east = dr[0], dr[1], dc[0], dc[1]
@@ -504,7 +504,7 @@
             copy.start()
 
     def first_step(idx, carry):
-        b = lax.rem(idx + 1, nb)
+        b = jnp.where(idx < 2, 1 - idx, idx)
         wait_rims(0, b, 4)
         place(0, b, ntr + 1)
         faces(b)
@@ -522,8 +522,7 @@
 
     lax.fori_loop(0, nb, first_step, 0)
 
-    def second_step(idx, carry):
-        b = jnp.where(idx < 2, 1 - idx, idx)
+    def second_step(b, carry):
         wait_rims(1, b, 3)
         place(1, b, ntr)
         advect(1, b)
@@ -552,6 +551,18 @@
     landed = nt(high, oh[...]) + nt(low, oh[...])
     for r in range(surf_out.shape[0]):
         surf_out[r : r + 1, :] = landed[0:1, r * LANES : (r + 1) * LANES]
+
+
+def export(tracers, surface, tracers_out, surface_out, sems):
+    copies = [
+        pltpu.make_async_copy(tracers.at[t], tracers_out.at[t], sems.at[t])
+        for t in range(tracers.shape[0])
+    ]
+    copies.append(pltpu.make_async_copy(surface, surface_out, sems.at[len(copies)]))
+    for copy in copies:
+        copy.start()
+    for copy in copies:
+        copy.wait()
 
 
 def body(
@@ -633,7 +644,7 @@
         dma((near,)),
         dma((near,)),
     ]
-    return pl.pallas_call(
+    results = pl.pallas_call(
         functools.partial(kernel, nty, ntx),
         out_shape=(
             pltpu.VMEM(tracers.shape, F32),
@@ -660,6 +671,19 @@
         peer_count,
         send_count,
     )
+    anywhere = pl.BlockSpec(memory_space=pl.ANY)
+    return pl.pallas_call(
+        export,
+        out_shape=(
+            jax.ShapeDtypeStruct(tracers.shape, F32),
+            jax.ShapeDtypeStruct(atm_flux.shape[1:], F32),
+        ),
+        in_specs=[pl.BlockSpec(memory_space=pl.ANY)] * 2,
+        out_specs=(anywhere, anywhere),
+        scratch_shapes=[dma((ntr + 1,))],
+        compiler_params=pltpu.CompilerParams(has_side_effects=True, vmem_limit_bytes=1024 * 1024),
+        name="export",
+    )(*results)
 
 
 def solution(mesh):

time: 38.8 us -> 36.9 us (0.951)
  the two profiles are of different devices: /device:TPU:0 before, /device:TPU:8 now
where the time goes in v4:
time: 36.9 us; the launch traced here: 36.7 us
  Pallas kernels  36.1 us (98%)
  between operations  0.64 us (2%)
    pallas_call x1, Pallas kernels, body(): pl.pallas_call(functools.partial(kernel, nty, ntx), out_shape=(pltpu.VMEM...  34.5 us
    pallas_call x1, Pallas kernels, body(): pl.pallas_call(export, out_shape=(jax.ShapeDtypeStruct(tracers.shape, F32...  1.63 us

profile of v4, /device:TPU:8, one launch (start us, length us, event | category | flops | bytes accessed | tf_op | source)
XLA Modules:
  0.0 36.7 jit_solution(5817628703161013167)
XLA Ops:
  0.6 34.5 %interval.1 = (f32[3,60,16,256]{3,2,1,0:T(8,128)S(1)}, f32[4,128]{1,0:T(4,128)S(1)}) custom-call(f32[3,60,16,256]{3,2,1,0:T(8,128)} %tracers.1, f32[2,60,16,256]{3,2,1,0:T(8,128)} %courant.1, bf16[4,15,15,16,256]{4,3,2,1,0:T(8,128)(2,1)} %mix.1, bf16[5,128,16,256]{3,2,1,0:T(8,128)(2,1)} %to_ocean.1, bf16[5,128,16,256]{3,2,1,0:T(8,128)(2,1)} %to_atmos.1, ...), custom_call_target="tpu_custom_call" | custom-call | flops 1000000000 | bytes 26000000 | tf_op jit(solution)/shard_map/interval/pallas_call | solution.py:647
  35.1 1.6 %export.1 = (f32[3,60,16,256]{3,2,1,0:T(8,128)}, f32[4,128]{1,0:T(4,128)}) custom-call(f32[3,60,16,256]{3,2,1,0:T(8,128)S(1)} %get-tuple-element.4.tracers, f32[4,128]{1,0:T(4,128)S(1)} %get-tuple-element.5.surface), custom_call_target="tpu_custom_call" | custom-call | tf_op jit(solution)/shard_map/export/pallas_call | solution.py:675

commit v5 on v4

--- a/solution.py
+++ b/solution.py
@@ -15,7 +15,7 @@
 LANES = 128
 RIM = 32
 ROWS = 256
-RGROUP = 5
+RGROUP = 3
 PAD = 32
 TOP = 8
 NEAR = tuple((di, dj) for di in (-1, 0, 1) for dj in (-1, 0, 1))
@@ -142,7 +142,10 @@
         )
     ]
     small[0].start()
-    order = (1, 0) + tuple(range(2, nb))
+    order = (1, 2, 0) + tuple(range(3, nb))
+
+    def nth(idx):
+        return jnp.where(idx < 2, idx + 1, jnp.where(idx == 2, 0, idx))
 
     def loads(b, first):
         made = []
@@ -171,9 +174,10 @@
             copy.start()
     for copy in small[1:]:
         copy.start()
-    pltpu.make_async_copy(mix.at[order[0]], mixv.at[order[0]], s_mix.at[order[0]]).start()
+    for b in order[:2]:
+        pltpu.make_async_copy(mix.at[b], mixv.at[b], s_mix.at[b]).start()
     pltpu.make_async_copy(to_ocean, toc, s_toc).start()
-    for b in order[1:]:
+    for b in order[2:]:
         pltpu.make_async_copy(mix.at[b], mixv.at[b], s_mix.at[b]).start()
     pltpu.make_async_copy(to_atmos, toa, s_toa).start()
 
@@ -298,7 +302,7 @@
     send(0, order[0], 4)
 
     def fill_and_send(idx, carry):
-        b = jnp.where(idx < 2, 1 - idx, idx)
+        b = nth(idx)
         fill(b)
         send(0, b, 4)
         return carry
@@ -490,21 +494,18 @@
         diagonal = (x & 15) == y
         rows = []
         for p in range(peers):
-            sums = nt(surface, toa[p].reshape(slots * oy, ox))
-            rows.append(jnp.sum(jnp.where(diagonal, sums, 0.0), axis=0, keepdims=True))
-        rows.append(jnp.zeros((8 - peers, slots * oy), F32))
-        sums = jnp.concatenate(rows, axis=0)
-        high = sums.astype(BF16)
-        low = (sums - high.astype(F32)).astype(BF16)
-        both = nn(jnp.concatenate([high, low], axis=0), c_et[...])
-        both = both[0:8] + both[8:16]
+            sums = jnp.where(diagonal, nt(surface, toa[p].reshape(slots * oy, ox)), 0.0)
+            high = sums.astype(BF16)
+            rows += [high, (sums - high.astype(F32)).astype(BF16)]
+        both = nn(jnp.concatenate(rows, axis=0), c_et[...])
+        both = jnp.sum(both.reshape(peers, 2 * oy, slots), axis=1)
         for p in range(peers):
             rt_s[p] = jnp.broadcast_to(both[p : p + 1], (8, slots))
         for copy in ret_copies():
             copy.start()
 
     def first_step(idx, carry):
-        b = jnp.where(idx < 2, 1 - idx, idx)
+        b = nth(idx)
         wait_rims(0, b, 4)
         place(0, b, ntr + 1)
         faces(b)
@@ -522,7 +523,8 @@
 
     lax.fori_loop(0, nb, first_step, 0)
 
-    def second_step(b, carry):
+    def second_step(idx, carry):
+        b = jnp.where(idx < 2, 1 - idx, idx)
         wait_rims(1, b, 3)
         place(1, b, ntr)
         advect(1, b)
@@ -548,7 +550,8 @@
     values = jnp.concatenate(parts, axis=1)
     high = values.astype(BF16)
     low = (values - high.astype(F32)).astype(BF16)
-    landed = nt(high, oh[...]) + nt(low, oh[...])
+    landed = nt(jnp.concatenate([high, low], axis=0), oh[...])
+    landed = landed[0:8] + landed[8:16]
     for r in range(surf_out.shape[0]):
         surf_out[r : r + 1, :] = landed[0:1, r * LANES : (r + 1) * LANES]
 

time: 36.9 us -> 36.5 us (0.989)
  the two profiles are of different devices: /device:TPU:8 before, /device:TPU:1 now
where the time goes in v5:
time: 36.5 us; the launch traced here: 36.4 us
  Pallas kernels  35.7 us (98%)
  between operations  0.64 us (2%)
    pallas_call x1, Pallas kernels, body(): pl.pallas_call(functools.partial(kernel, nty, ntx), out_shape=(pltpu.VMEM...  34.1 us
    pallas_call x1, Pallas kernels, body(): pl.pallas_call(export, out_shape=(jax.ShapeDtypeStruct(tracers.shape, F32...  1.63 us

profile of v5, /device:TPU:1, one launch (start us, length us, event | category | flops | bytes accessed | tf_op | source)
XLA Modules:
  0.0 36.4 jit_solution(7059223008229766877)
XLA Ops:
  0.6 34.1 %interval.1 = (f32[3,60,16,256]{3,2,1,0:T(8,128)S(1)}, f32[4,128]{1,0:T(4,128)S(1)}) custom-call(f32[3,60,16,256]{3,2,1,0:T(8,128)} %tracers.1, f32[2,60,16,256]{3,2,1,0:T(8,128)} %courant.1, bf16[4,15,15,16,256]{4,3,2,1,0:T(8,128)(2,1)} %mix.1, bf16[5,128,16,256]{3,2,1,0:T(8,128)(2,1)} %to_ocean.1, bf16[5,128,16,256]{3,2,1,0:T(8,128)(2,1)} %to_atmos.1, ...), custom_call_target="tpu_custom_call" | custom-call | flops 1000000000 | bytes 26000000 | tf_op jit(solution)/shard_map/interval/pallas_call | solution.py:650
  34.7 1.6 %export.1 = (f32[3,60,16,256]{3,2,1,0:T(8,128)}, f32[4,128]{1,0:T(4,128)}) custom-call(f32[3,60,16,256]{3,2,1,0:T(8,128)S(1)} %get-tuple-element.4.tracers, f32[4,128]{1,0:T(4,128)S(1)} %get-tuple-element.5.surface), custom_call_target="tpu_custom_call" | custom-call | tf_op jit(solution)/shard_map/export/pallas_call | solution.py:678

commit v6 on v5

--- a/solution.py
+++ b/solution.py
@@ -141,11 +141,10 @@
             )
         )
     ]
-    small[0].start()
-    order = (1, 2, 0) + tuple(range(3, nb))
+    order = (1, 0) + tuple(range(2, nb))
 
     def nth(idx):
-        return jnp.where(idx < 2, idx + 1, jnp.where(idx == 2, 0, idx))
+        return jnp.where(idx < 2, 1 - idx, idx)
 
     def loads(b, first):
         made = []
@@ -169,15 +168,14 @@
             ]
         return made
 
+    for copy in small:
+        copy.start()
     for b in order:
         for copy in loads(b, b * zb):
             copy.start()
-    for copy in small[1:]:
-        copy.start()
-    for b in order[:2]:
-        pltpu.make_async_copy(mix.at[b], mixv.at[b], s_mix.at[b]).start()
+    pltpu.make_async_copy(mix.at[order[0]], mixv.at[order[0]], s_mix.at[order[0]]).start()
     pltpu.make_async_copy(to_ocean, toc, s_toc).start()
-    for b in order[2:]:
+    for b in order[1:]:
         pltpu.make_async_copy(mix.at[b], mixv.at[b], s_mix.at[b]).start()
     pltpu.make_async_copy(to_atmos, toa, s_toa).start()
 
@@ -284,31 +282,6 @@
         pack(0, b, ntr + 1, ntr + 1)
 
     tmp[...] = jnp.zeros_like(tmp)
-    fill(order[0])
-
-    for s in range(2):
-        @pl.when(jnp.logical_not(takes[s]))
-        def _():
-            hr[:, :, :, s * RIM : (s + 1) * RIM, :] = jnp.zeros((SUBSTEPS, nb, 4, RIM, ox), BF16)
-            dr[s] = jnp.zeros((8, ox), I32)
-
-        @pl.when(jnp.logical_not(takes[2 + s]))
-        def _():
-            hc[:, :, s * 8 : (s + 1) * 8, :] = jnp.zeros((SUBSTEPS, nb, 8, ox), F32)
-            dc[s] = jnp.zeros((oy, LANES), I32)
-
-    pl.semaphore_wait(barrier, len(NEAR) - 1)
-    start_all(depth_copies())
-    send(0, order[0], 4)
-
-    def fill_and_send(idx, carry):
-        b = nth(idx)
-        fill(b)
-        send(0, b, 4)
-        return carry
-
-    lax.fori_loop(1, nb, fill_and_send, 0)
-
     for copy in small[1:]:
         copy.wait()
 
@@ -325,9 +298,33 @@
     picks = nn(flat[...].astype(BF16), oh[...])
     for k in range(len(NEAR)):
         pk_s[k] = picks[:, k * slots : (k + 1) * slots]
-
+    fill(order[0])
+
+    for s in range(2):
+        @pl.when(jnp.logical_not(takes[s]))
+        def _():
+            hr[:, :, :, s * RIM : (s + 1) * RIM, :] = jnp.zeros((SUBSTEPS, nb, 4, RIM, ox), BF16)
+            dr[s] = jnp.zeros((8, ox), I32)
+
+        @pl.when(jnp.logical_not(takes[2 + s]))
+        def _():
+            hc[:, :, s * 8 : (s + 1) * 8, :] = jnp.zeros((SUBSTEPS, nb, 8, ox), F32)
+            dc[s] = jnp.zeros((oy, LANES), I32)
+
+    pl.semaphore_wait(barrier, len(NEAR) - 1)
+    start_all(depth_copies())
+    send(0, order[0], 4)
     for copy in near_copies(pk_s, pk_r, pk_ss, pk_rs, lambda k, di, dj: k):
         copy.start()
+
+    def fill_and_send(idx, carry):
+        b = nth(idx)
+        fill(b)
+        send(0, b, 4)
+        return carry
+
+    lax.fori_loop(1, nb, fill_and_send, 0)
+
 
     g = iota((ox, 2 * ox), 0)
     n = iota((ox, 2 * ox), 1)
@@ -523,8 +520,7 @@
 
     lax.fori_loop(0, nb, first_step, 0)
 
-    def second_step(idx, carry):
-        b = jnp.where(idx < 2, 1 - idx, idx)
+    def second_step(b, carry):
         wait_rims(1, b, 3)
         place(1, b, ntr)
         advect(1, b)

time: 36.5 us -> 35.7 us (0.978)
  the two profiles are of different devices: /device:TPU:1 before, /device:TPU:8 now
where the time goes in v6:
time: 35.7 us; the launch traced here: 35.5 us
  Pallas kernels  34.9 us (98%)
  between operations  0.64 us (2%)
    pallas_call x1, Pallas kernels, body(): pl.pallas_call(functools.partial(kernel, nty, ntx), out_shape=(pltpu.VMEM...  33.2 us
    pallas_call x1, Pallas kernels, body(): pl.pallas_call(export, out_shape=(jax.ShapeDtypeStruct(tracers.shape, F32...  1.63 us

profile of v6, /device:TPU:8, one launch (start us, length us, event | category | flops | bytes accessed | tf_op | source)
XLA Modules:
  0.0 35.5 jit_solution(17074814508797012586)
XLA Ops:
  0.6 33.2 %interval.1 = (f32[3,60,16,256]{3,2,1,0:T(8,128)S(1)}, f32[4,128]{1,0:T(4,128)S(1)}) custom-call(f32[3,60,16,256]{3,2,1,0:T(8,128)} %tracers.1, f32[2,60,16,256]{3,2,1,0:T(8,128)} %courant.1, bf16[4,15,15,16,256]{4,3,2,1,0:T(8,128)(2,1)} %mix.1, bf16[5,128,16,256]{3,2,1,0:T(8,128)(2,1)} %to_ocean.1, bf16[5,128,16,256]{3,2,1,0:T(8,128)(2,1)} %to_atmos.1, ...), custom_call_target="tpu_custom_call" | custom-call | flops 1000000000 | bytes 26000000 | tf_op jit(solution)/shard_map/interval/pallas_call | solution.py:646
  33.9 1.6 %export.1 = (f32[3,60,16,256]{3,2,1,0:T(8,128)}, f32[4,128]{1,0:T(4,128)}) custom-call(f32[3,60,16,256]{3,2,1,0:T(8,128)S(1)} %get-tuple-element.4.tracers, f32[4,128]{1,0:T(4,128)S(1)} %get-tuple-element.5.surface), custom_call_target="tpu_custom_call" | custom-call | tf_op jit(solution)/shard_map/export/pallas_call | solution.py:674

commit v7 on v6

--- a/solution.py
+++ b/solution.py
@@ -298,6 +298,9 @@
     picks = nn(flat[...].astype(BF16), oh[...])
     for k in range(len(NEAR)):
         pk_s[k] = picks[:, k * slots : (k + 1) * slots]
+    pl.semaphore_wait(barrier, len(NEAR) - 1)
+    for copy in near_copies(pk_s, pk_r, pk_ss, pk_rs, lambda k, di, dj: k):
+        copy.start()
     fill(order[0])
 
     for s in range(2):
@@ -311,11 +314,8 @@
             hc[:, :, s * 8 : (s + 1) * 8, :] = jnp.zeros((SUBSTEPS, nb, 8, ox), F32)
             dc[s] = jnp.zeros((oy, LANES), I32)
 
-    pl.semaphore_wait(barrier, len(NEAR) - 1)
     start_all(depth_copies())
     send(0, order[0], 4)
-    for copy in near_copies(pk_s, pk_r, pk_ss, pk_rs, lambda k, di, dj: k):
-        copy.start()
 
     def fill_and_send(idx, carry):
         b = nth(idx)
@@ -359,6 +359,8 @@
     depx[2] = pltpu.roll(tall, oy + 7, 0)[:oy]
     tall = jnp.concatenate([south, dep], axis=0)
     depx[3] = pltpu.roll(tall, 1, 0)[8:]
+    for a in range(4):
+        depx[a] = jnp.minimum(depx[a], dep)
 
     def wait_rims(step, b, fields):
         wait_all(rim_copies(step, b, fields))
@@ -382,8 +384,7 @@
             rows = slice(k * oy, (k + 1) * oy)
             for h in range(halves):
                 lanes = slice(h * LANES, (h + 1) * LANES)
-                wet = at < depth[:, lanes]
-                near_wet = [wet & (at < depx[a, :, lanes]) for a in range(4)]
+                near_wet = [at < depx[a, :, lanes] for a in range(4)]
                 x0 = cx[b, k, h]
                 y0 = qs[ntr, b, k, h, own, :]
                 others = (

time: 35.7 us -> 35.8 us (level)
  no operation moved by 1% of the time
where the time goes in v7:
time: 35.8 us; the launch traced here: 35.7 us
  Pallas kernels  35 us (98%)
  between operations  0.64 us (2%)
    pallas_call x1, Pallas kernels, body(): pl.pallas_call(functools.partial(kernel, nty, ntx), out_shape=(pltpu.VMEM...  33.4 us
    pallas_call x1, Pallas kernels, body(): pl.pallas_call(export, out_shape=(jax.ShapeDtypeStruct(tracers.shape, F32...  1.63 us

profile of v7, /device:TPU:8, one launch (start us, length us, event | category | flops | bytes accessed | tf_op | source)
XLA Modules:
  0.0 35.7 jit_solution(3611182273229870804)
XLA Ops:
  0.6 33.4 %interval.1 = (f32[3,60,16,256]{3,2,1,0:T(8,128)S(1)}, f32[4,128]{1,0:T(4,128)S(1)}) custom-call(f32[3,60,16,256]{3,2,1,0:T(8,128)} %tracers.1, f32[2,60,16,256]{3,2,1,0:T(8,128)} %courant.1, bf16[4,15,15,16,256]{4,3,2,1,0:T(8,128)(2,1)} %mix.1, bf16[5,128,16,256]{3,2,1,0:T(8,128)(2,1)} %to_ocean.1, bf16[5,128,16,256]{3,2,1,0:T(8,128)(2,1)} %to_atmos.1, ...), custom_call_target="tpu_custom_call" | custom-call | flops 1000000000 | bytes 26000000 | tf_op jit(solution)/shard_map/interval/pallas_call | solution.py:647
  34.0 1.6 %export.1 = (f32[3,60,16,256]{3,2,1,0:T(8,128)}, f32[4,128]{1,0:T(4,128)}) custom-call(f32[3,60,16,256]{3,2,1,0:T(8,128)S(1)} %get-tuple-element.4.tracers, f32[4,128]{1,0:T(4,128)S(1)} %get-tuple-element.5.surface), custom_call_target="tpu_custom_call" | custom-call | tf_op jit(solution)/shard_map/export/pallas_call | solution.py:675
